TPU v7x, 32 devices: a whole 2x2x4 slice. The times are simulated.
32 devices in a mesh: row: 2 (over y), col: 4 (over x, core), dp: 4 (over z).
Axes of the slice: x: 2, y: 2, z: 4, core: 2. Of those that a mesh axis runs over, the one named last changes fastest.
Arguments:
- image: bfloat16 [4, 256, 48, 512], P('dp', None, 'row', 'col'), may hold values from -6 to 6
- labels: int32 [4, 2, 8], P('dp', 'row', 'col'), may hold values from 0 to 7
- weights: float32 [141312], replicated, may hold values from -0.375 to 0.375
- momentum: float32 [141312], P(('row', 'col', 'dp')), may hold values from -0.006 to 0.006
Outputs:
- new_weights: float32 [141312], P(('row', 'col', 'dp'))
- new_momentum: float32 [141312], P(('row', 'col', 'dp'))
- update: float32 [141312], P(('row', 'col', 'dp'))
- loss: float32 [], replicated
All inputs are finite; a program needn't handle non-finite values. Where the computation divides by a largest or mean magnitude, that divisor is 1e-20 or more.
Results may differ from a plain program's by a relative error of at most 0.0011.
Values may be sent and summed in bfloat16 or wider, within the bound.
A program may use at most 64 MiB of HBM per device.

v0:
```python
import jax
import jax.numpy as jnp
from jax import lax
from jax.sharding import PartitionSpec as P

C = 256
MID = 64
CLASSES = 8
TILE_ROWS = 24
TILE_COLS = 64


beta_one = 0.9
beta_two = 0.99
learn_rate = 0.0001
weight_decay = 0.1


def extended(block, sides, width):
    for axis, dim in sides:
        count = lax.axis_size(axis)
        forward = [(i, i + 1) for i in range(count - 1)]
        backward = [(target, source) for source, target in forward]
        low = lax.ppermute(
            lax.slice_in_dim(block, block.shape[dim] - width, None, axis=dim), axis, forward
        )
        high = lax.ppermute(lax.slice_in_dim(block, 0, width, axis=dim), axis, backward)
        block = jnp.concatenate([low, block, high], axis=dim)
    return block


def unpack(weights):
    offset = 0
    blocks_list = []
    for number in range(2):
        w_in = weights[offset : offset + C * MID].reshape(C, MID)
        offset = offset + C * MID
        w_mid = weights[offset : offset + 9 * MID * MID].reshape(9, MID, MID)
        offset = offset + 9 * MID * MID
        w_out = weights[offset : offset + MID * C].reshape(MID, C)
        offset = offset + MID * C
        blocks_list.append(
            (w_in.astype(jnp.bfloat16), w_mid.astype(jnp.bfloat16), w_out.astype(jnp.bfloat16))
        )
    head = weights[offset:].reshape(C, CLASSES)
    return (blocks_list, head)


def forward_rim(field):
    return extended(field, (("row", 1), ("col", 2)), 1)


def backward_rim(field):
    return extended(field, (("row", 1), ("col", 2)), 1)


def conv_taps(w_mid, padded, height, width):
    total = jnp.zeros((w_mid.shape[2], height, width), jnp.float32)
    for position in range(9):
        shift_row = position // 3
        shift_col = position % 3
        total = total + jnp.einsum(
            "io,ihw->ohw",
            w_mid[position],
            padded[:, shift_row : shift_row + height, shift_col : shift_col + width],
            preferred_element_type=jnp.float32,
        )
    return total


def local(image, labels, weights, momentum):
    inputs = image[0]
    label_grid = labels[0]
    height, width = (inputs.shape[1], inputs.shape[2])
    blocks_list, head = unpack(weights)
    total_tiles = (
        label_grid.shape[0]
        * label_grid.shape[1]
        * lax.axis_size("row")
        * lax.axis_size("col")
        * lax.axis_size("dp")
    )
    stored = []
    for w_in, w_mid, w_out in blocks_list:
        h_first = jnp.maximum(
            jnp.einsum("io,ihw->ohw", w_in, inputs, preferred_element_type=jnp.float32), 0.0
        ).astype(jnp.bfloat16)
        padded = forward_rim(h_first)
        h_second = jnp.maximum(conv_taps(w_mid, padded, height, width), 0.0).astype(jnp.bfloat16)
        output = jnp.maximum(
            jnp.einsum("io,ihw->ohw", w_out, h_second, preferred_element_type=jnp.float32)
            + inputs.astype(jnp.float32),
            0.0,
        ).astype(jnp.bfloat16)
        kept = padded
        stored.append((inputs, kept, h_second, output))
        inputs = output
    tiles_a = height // TILE_ROWS
    tiles_b = width // TILE_COLS
    pooled = jnp.mean(
        inputs.astype(jnp.float32).reshape(C, tiles_a, TILE_ROWS, tiles_b, TILE_COLS), axis=(2, 4)
    )
    logits = jnp.einsum("cab,ck->abk", pooled, head, precision=lax.Precision.HIGHEST)
    highest = jnp.max(logits, axis=-1, keepdims=True)
    logsum = jnp.log(jnp.sum(jnp.exp(logits - highest), axis=-1, keepdims=True)) + highest
    onehot = (label_grid[:, :, None] == jnp.arange(CLASSES, dtype=jnp.int32)).astype(jnp.float32)
    loss_part = jnp.sum(logsum[:, :, 0] - jnp.sum(onehot * logits, axis=-1))
    dlogits = (jnp.exp(logits - logsum) - onehot) / total_tiles
    grad_head = jnp.einsum("cab,abk->ck", pooled, dlogits, precision=lax.Precision.HIGHEST)
    dpooled = jnp.einsum("abk,ck->cab", dlogits, head, precision=lax.Precision.HIGHEST) / (
        TILE_ROWS * TILE_COLS
    )
    upstream = (
        jnp.broadcast_to(dpooled[:, :, None, :, None], (C, tiles_a, TILE_ROWS, tiles_b, TILE_COLS))
        .reshape(C, height, width)
        .astype(jnp.bfloat16)
    )
    grads = [None, None]
    for number in (1, 0):
        w_in, w_mid, w_out = blocks_list[number]
        inputs, kept, h_second, output = stored[number]
        padded = kept
        d_sum = jnp.where(output > 0, upstream, jnp.zeros_like(upstream))
        grad_out = jnp.einsum("ihw,ohw->io", h_second, d_sum, preferred_element_type=jnp.float32)
        d_second = jnp.einsum("io,ohw->ihw", w_out, d_sum, preferred_element_type=jnp.float32)
        d_second = jnp.where(h_second > 0, d_second, 0.0).astype(jnp.bfloat16)
        spread_back = backward_rim(d_second)
        grad_mid = jnp.stack(
            [
                jnp.einsum(
                    "ihw,ohw->io",
                    padded[
                        :,
                        position // 3 : position // 3 + height,
                        position % 3 : position % 3 + width,
                    ],
                    d_second,
                    preferred_element_type=jnp.float32,
                )
                for position in range(9)
            ]
        )
        d_first = jnp.zeros((MID, height, width), jnp.float32)
        for position in range(9):
            shift_row = 2 - position // 3
            shift_col = 2 - position % 3
            d_first = d_first + jnp.einsum(
                "io,ohw->ihw",
                w_mid[position],
                spread_back[:, shift_row : shift_row + height, shift_col : shift_col + width],
                preferred_element_type=jnp.float32,
            )
        h_first = padded[:, 1:-1, 1:-1]
        d_first = jnp.where(h_first > 0, d_first, 0.0).astype(jnp.bfloat16)
        grad_in = jnp.einsum("ihw,ohw->io", inputs, d_first, preferred_element_type=jnp.float32)
        if number == 1:
            upstream = (
                jnp.einsum("io,ohw->ihw", w_in, d_first, preferred_element_type=jnp.float32)
                + d_sum.astype(jnp.float32)
            ).astype(jnp.bfloat16)
        grads[number] = jnp.concatenate([grad_in.ravel(), grad_mid.ravel(), grad_out.ravel()])
    flat = jnp.concatenate([grads[0], grads[1], grad_head.ravel()])
    share = momentum.shape[0]
    start = lax.axis_index(("row", "col", "dp")) * share
    total = lax.psum(flat, ("row", "col", "dp"))
    grad = lax.dynamic_slice_in_dim(total, start, share, 0)
    weight_share = lax.dynamic_slice_in_dim(weights, start, share, 0)
    mixed = beta_one * momentum + (1.0 - beta_one) * grad
    abs_total, loss_total = lax.psum((jnp.sum(jnp.abs(mixed)), loss_part), ("row", "col", "dp"))
    scale_tau = abs_total / weights.shape[0] + 1e-06
    update = mixed / (jnp.abs(mixed) + scale_tau)
    new_weights = weight_share - learn_rate * (update + weight_decay * weight_share)
    new_momentum = beta_two * momentum + (1.0 - beta_two) * grad
    return (new_weights, new_momentum, update, loss_total / total_tiles)


def solution(mesh):
    in_specs = (P("dp", None, "row", "col"), P("dp", "row", "col"), P(), P(("row", "col", "dp")))
    out_specs = (P(("row", "col", "dp")), P(("row", "col", "dp")), P(("row", "col", "dp")), P())
    return jax.shard_map(local, mesh=mesh, in_specs=in_specs, out_specs=out_specs, check_vma=False)
```

profile of v0, /device:TPU:0, one launch (start us, length us, event | category | flops | bytes accessed | tf_op | source)
XLA Modules:
  0.0 334.8 jit_solution(14977379536267410052)
XLA Ops:
  7.2 1.1 convert.8
  9.7 2.1 copy.93
  11.9 2.3 convert_reduce_fusion.1
  14.8 5.5 %collective-permute-start = (bf16[64,1,128]{2,0,1:T(8,128)(2,1)}, bf16[64,1,128]{2,0,1:T(8,128)(2,1)}, u32[]{:S(2)}, u32[]{:S(2)}) collective-permute-start(bf16[64,1,128]{2,0,1:T(8,128)(2,1)} %get-tuple-element.35), channel_id=1, source_target_pairs={{0,16},{1,17},{2,18},{3,19},{4,20},{5,21},{6,22},{7,23},{8,24},{9,... | collective-permute-start | bytes 49160 | tf_op jit(solution)/shard_map/ppermute | solution.py:24
  20.3 1.3 collective-permute-start.1
  22.9 1.9 fusion.157
  24.8 1.6 and_convert_fusion
  26.6 1.9 copy.59
  40.1 0.8 pad_maximum_fusion.4
  41.2 1.5 collective-permute-start.2
  42.6 1.3 collective-permute-start.3
  44.0 1.0 fusion.139
  45.0 1.0 fusion.138
  46.0 1.8 collective-permute-done.3
  47.8 1.4 maximum_maximum_fusion
  51.8 0.9 copy-done.3
  54.0 5.1 %collective-permute-start.4 = (bf16[64,1,128]{2,0,1:T(8,128)(2,1)S(1)}, bf16[64,1,128]{2,0,1:T(8,128)(2,1)S(1)}, u32[]{:S(2)}, u32[]{:S(2)}) collective-permute-start(bf16[64,1,128]{2,0,1:T(8,128)(2,1)S(1)} %get-tuple-element.33), channel_id=1, source_target_pairs={{0,16},{1,17},{2,18},{3,19},{4,20},{5,21},{6,22},{7,23},{8,24},{9,... | collective-permute-start | bytes 49160 | tf_op jit(solution)/shard_map/ppermute | solution.py:24
  59.2 1.3 collective-permute-start.5
  60.8 4.0 %collective-permute-done.5 = bf16[64,1,128]{2,0,1:T(8,128)(2,1)S(1)} collective-permute-done((bf16[64,1,128]{2,0,1:T(8,128)(2,1)S(1)}, bf16[64,1,128]{2,0,1:T(8,128)(2,1)S(1)}, u32[]{:S(2)}, u32[]{:S(2)}) %collective-permute-start.5) | collective-permute-done | bytes 16416 | tf_op jit(solution)/shard_map/ppermute | solution.py:27
  65.1 6.8 %collective-permute-start.6 = (bf16[64,26,1]{2,0,1:T(8,128)(2,1)S(1)}, bf16[64,26,1]{2,0,1:T(8,128)(2,1)S(1)}, u32[]{:S(2)}, u32[]{:S(2)}) collective-permute-start(bf16[64,26,1]{2,0,1:T(8,128)(2,1)S(1)} %get-tuple-element.23), channel_id=1, source_target_pairs={{0,4},{4,8},{8,12},{1,5},{5,9},{9,13},{2,6},{6,10},{10,14},{3,7},{... | collective-permute-start | bytes 9992 | tf_op jit(solution)/shard_map/ppermute | solution.py:24
  71.9 1.5 collective-permute-start.7
  74.0 2.3 collective-permute-done.7
  79.2 0.8 convert_reduce_fusion
  85.8 1.3 collective-permute-start.9
  87.1 4.5 %collective-permute-start.8 = (bf16[64,1,128]{2,0,1:T(8,128)(2,1)S(1)}, bf16[64,1,128]{2,0,1:T(8,128)(2,1)S(1)}, u32[]{:S(2)}, u32[]{:S(2)}) collective-permute-start(bf16[64,1,128]{2,0,1:T(8,128)(2,1)S(1)} %get-tuple-element.31), channel_id=1, source_target_pairs={{0,16},{1,17},{2,18},{3,19},{4,20},{5,21},{6,22},{7,23},{8,24},{9,... | collective-permute-start | bytes 49160 | tf_op jit(solution)/shard_map/ppermute | solution.py:24
  91.7 1.1 fusion.197
  94.6 1.1 reshape.196
  96.0 1.3 collective-permute-start.10
  97.3 8.5 %collective-permute-start.11 = (bf16[64,26,1]{2,0,1:T(8,128)(2,1)S(1)}, bf16[64,26,1]{2,0,1:T(8,128)(2,1)S(1)}, u32[]{:S(2)}, u32[]{:S(2)}) collective-permute-start(bf16[64,26,1]{2,0,1:T(8,128)(2,1)S(1)} %get-tuple-element.20), channel_id=1, source_target_pairs={{0,4},{4,8},{8,12},{1,5},{5,9},{9,13},{2,6},{6,10},{10,14},{3,7},{... | collective-permute-start | bytes 9992 | tf_op jit(solution)/shard_map/ppermute | solution.py:24
  110.1 1.0 copy-done.12
  114.5 1.0 fusion.53
  116.9 1.0 fusion.52
  118.2 1.3 collective-permute-start.13
  119.5 4.5 %collective-permute-start.12 = (bf16[64,1,128]{2,0,1:T(8,128)(2,1)}, bf16[64,1,128]{2,0,1:T(8,128)(2,1)S(1)}, u32[]{:S(2)}, u32[]{:S(2)}) collective-permute-start(bf16[64,1,128]{2,0,1:T(8,128)(2,1)} %get-tuple-element.29), channel_id=1, source_target_pairs={{0,16},{1,17},{2,18},{3,19},{4,20},{5,21},{6,22},{7,23},{8,24},{9,... | collective-permute-start | bytes 49160 | tf_op jit(solution)/shard_map/ppermute | solution.py:24
  124.0 1.1 fusion.198
  125.6 1.1 reshape.193
  127.7 1.3 collective-permute-start.14
  129.0 7.4 %collective-permute-start.15 = (bf16[64,26,1]{2,0,1:T(8,128)(2,1)S(1)}, bf16[64,26,1]{2,0,1:T(8,128)(2,1)S(1)}, u32[]{:S(2)}, u32[]{:S(2)}) collective-permute-start(bf16[64,26,1]{2,0,1:T(8,128)(2,1)S(1)} %get-tuple-element.16), channel_id=1, source_target_pairs={{0,4},{4,8},{8,12},{1,5},{5,9},{9,13},{2,6},{6,10},{10,14},{3,7},{... | collective-permute-start | bytes 9992 | tf_op jit(solution)/shard_map/ppermute | solution.py:24
  136.7 1.1 fusion.76
  138.9 1.2 fusion.78
  140.3 1.2 fusion.74
  141.5 1.3 fusion.13
  143.1 2.4 fusion.49
  145.9 0.8 copy-done.16
  146.7 134.5 %all-reduce.3.cloned.1.call-done = f32[141312]{0:T(1024)} async-done(((f32[141312]{0:T(1024)}), f32[141312]{0:T(1024)}) %all-reduce.3.cloned.1.call-update) | async-done | bytes 565264 | tf_op jit(solution)/shard_map/psum | solution.py:165
  281.2 1.4 abs_reduce_fusion
  282.7 41.4 %all-reduce = (f32[]{:T(128)}, f32[]{:T(128)}) all-reduce(f32[]{:T(128)} %abs_reduce_fusion, f32[]{:T(128)} %get-tuple-element.10), channel_id=1, replica_groups=mesh['row'=2,'col'=4,'dp'=4] {'row','col','dp'}, use_global_device_ids=true, to_apply=%region_6.7 | all-reduce | flops 2 | bytes 16 | tf_op jit(solution)/shard_map/psum | solution.py:169
  325.4 1.5 multiply_subtract_fusion
  (265 shorter events, 43.5 us)
Async XLA Ops:
  7.2 274.1 %all-reduce.3.cloned.1.call-start = ((), (), s32[]{:S(2)}) async-start(), calls=%async_computation | async-start | bytes 1130496 | tf_op jit(solution)/shard_map/psum | solution.py:165
  11.9 13.0 %copy-start = (bf16[256,24,128]{0,2,1:T(8,128)(2,1)}, bf16[256,24,128]{0,2,1:T(8,128)(2,1)S(1)}, u32[]{:S(2)}) copy-start(bf16[256,24,128]{0,2,1:T(8,128)(2,1)S(1)} %copy.93) | copy-start | bytes 4718596
  11.9 9.7 %copy-start.14 = (bf16[141312]{0:T(1024)(128)(2,1)S(1)}, bf16[141312]{0:T(1024)(128)(2,1)}, u32[]{:S(2)}) copy-start(bf16[141312]{0:T(1024)(128)(2,1)} %copy-done.13) | copy-start | bytes 847876
  11.9 14.5 %copy-start.2 = (bf16[1,256,24,128]{3,2,1,0:T(8,128)(2,1)S(1)}, bf16[1,256,24,128]{3,2,1,0:T(8,128)(2,1)}, u32[]{:S(2)}) copy-start(bf16[1,256,24,128]{3,2,1,0:T(8,128)(2,1)} %param.4) | copy-start | bytes 4718596
  14.8 25.3 %collective-permute-start = (bf16[64,1,128]{2,0,1:T(8,128)(2,1)}, bf16[64,1,128]{2,0,1:T(8,128)(2,1)}, u32[]{:S(2)}, u32[]{:S(2)}) collective-permute-start(bf16[64,1,128]{2,0,1:T(8,128)(2,1)} %get-tuple-element.35), channel_id=1, source_target_pairs={{0,16},{1,17},{2,18},{3,19},{4,20},{5,21},{6,22},{7,23},{8,24},{9,... | collective-permute-start | bytes 49160 | tf_op jit(solution)/shard_map/ppermute | solution.py:24
  20.3 19.9 %collective-permute-start.1 = (bf16[64,1,128]{2,0,1:T(8,128)(2,1)}, bf16[64,1,128]{2,0,1:T(8,128)(2,1)}, u32[]{:S(2)}, u32[]{:S(2)}) collective-permute-start(bf16[64,1,128]{2,0,1:T(8,128)(2,1)} %get-tuple-element.36), channel_id=1, source_target_pairs={{16,0},{17,1},{18,2},{19,3},{20,4},{21,5},{22,6},{23,7},{24,8},{25... | collective-permute-start | bytes 49160 | tf_op jit(solution)/shard_map/ppermute | solution.py:27
  26.5 2.8 copy-start.42
  26.5 3.0 copy-start.41
  26.5 3.2 copy-start.40
  26.5 3.3 copy-start.39
  26.5 4.1 %copy-start.38 = (bf16[4096]{0:T(1024)(128)(2,1)S(1)}, bf16[4096]{0:T(1024)(128)(2,1)}, u32[]{:S(2)}) copy-start(bf16[4096]{0:T(1024)(128)(2,1)} %get-tuple-element.39) | copy-start | bytes 24580
  26.5 4.8 %copy-start.37 = (bf16[4096]{0:T(1024)(128)(2,1)S(1)}, bf16[4096]{0:T(1024)(128)(2,1)}, u32[]{:S(2)}) copy-start(bf16[4096]{0:T(1024)(128)(2,1)} %get-tuple-element.40) | copy-start | bytes 24580
  26.5 5.6 %copy-start.36 = (bf16[4096]{0:T(1024)(128)(2,1)S(1)}, bf16[4096]{0:T(1024)(128)(2,1)}, u32[]{:S(2)}) copy-start(bf16[4096]{0:T(1024)(128)(2,1)} %get-tuple-element.38) | copy-start | bytes 24580
  26.5 6.3 %copy-start.35 = (bf16[4096]{0:T(1024)(128)(2,1)S(1)}, bf16[4096]{0:T(1024)(128)(2,1)}, u32[]{:S(2)}) copy-start(bf16[4096]{0:T(1024)(128)(2,1)} %get-tuple-element.37) | copy-start | bytes 24580
  26.5 7.1 %copy-start.34 = (bf16[4096]{0:T(1024)(128)(2,1)S(1)}, bf16[4096]{0:T(1024)(128)(2,1)}, u32[]{:S(2)}) copy-start(bf16[4096]{0:T(1024)(128)(2,1)} %get-tuple-element.53) | copy-start | bytes 24580
  26.5 7.9 %copy-start.33 = (bf16[4096]{0:T(1024)(128)(2,1)S(1)}, bf16[4096]{0:T(1024)(128)(2,1)}, u32[]{:S(2)}) copy-start(bf16[4096]{0:T(1024)(128)(2,1)} %get-tuple-element.51) | copy-start | bytes 24580
  26.5 8.6 %copy-start.32 = (bf16[4096]{0:T(1024)(128)(2,1)S(1)}, bf16[4096]{0:T(1024)(128)(2,1)}, u32[]{:S(2)}) copy-start(bf16[4096]{0:T(1024)(128)(2,1)} %get-tuple-element.52) | copy-start | bytes 24580
  26.5 9.4 %copy-start.31 = (bf16[4096]{0:T(1024)(128)(2,1)S(1)}, bf16[4096]{0:T(1024)(128)(2,1)}, u32[]{:S(2)}) copy-start(bf16[4096]{0:T(1024)(128)(2,1)} %copy-done.30) | copy-start | bytes 24580
  26.6 9.4 %copy-start.29 = (bf16[4096]{0:T(1024)(128)(2,1)S(1)}, bf16[4096]{0:T(1024)(128)(2,1)}, u32[]{:S(2)}) copy-start(bf16[4096]{0:T(1024)(128)(2,1)} %get-tuple-element.54) | copy-start | bytes 24580
  26.6 10.2 %copy-start.28 = (bf16[4096]{0:T(1024)(128)(2,1)S(1)}, bf16[4096]{0:T(1024)(128)(2,1)}, u32[]{:S(2)}) copy-start(bf16[4096]{0:T(1024)(128)(2,1)} %get-tuple-element.47) | copy-start | bytes 24580
  26.6 11.0 %copy-start.27 = (bf16[4096]{0:T(1024)(128)(2,1)S(1)}, bf16[4096]{0:T(1024)(128)(2,1)}, u32[]{:S(2)}) copy-start(bf16[4096]{0:T(1024)(128)(2,1)} %get-tuple-element.48) | copy-start | bytes 24580
  26.6 11.7 %copy-start.26 = (bf16[4096]{0:T(1024)(128)(2,1)S(1)}, bf16[4096]{0:T(1024)(128)(2,1)}, u32[]{:S(2)}) copy-start(bf16[4096]{0:T(1024)(128)(2,1)} %get-tuple-element.46) | copy-start | bytes 24580
  26.6 13.2 %copy-start.24 = (bf16[16384]{0:T(1024)(128)(2,1)S(1)}, bf16[16384]{0:T(1024)(128)(2,1)}, u32[]{:S(2)}) copy-start(bf16[16384]{0:T(1024)(128)(2,1)} %get-tuple-element.57) | copy-start | bytes 98308
  26.6 13.3 %copy-start.22 = (bf16[16384]{0:T(1024)(128)(2,1)S(1)}, bf16[16384]{0:T(1024)(128)(2,1)}, u32[]{:S(2)}) copy-start(bf16[16384]{0:T(1024)(128)(2,1)} %get-tuple-element.55) | copy-start | bytes 98308
  26.6 13.4 %copy-start.23 = (bf16[16384]{0:T(1024)(128)(2,1)S(1)}, bf16[16384]{0:T(1024)(128)(2,1)}, u32[]{:S(2)}) copy-start(bf16[16384]{0:T(1024)(128)(2,1)} %get-tuple-element.56) | copy-start | bytes 98308
  26.6 13.4 %slice-start = ((f32[141312]{0:T(1024)}), f32[2048]{0:T(1024)S(1)}, s32[]{:S(2)}) async-start(f32[141312]{0:T(1024)} %param.6), calls=%async_computation.1 | async-start | bytes 16384 | tf_op jit(solution)/shard_map/slice | solution.py:45
  41.2 4.9 %collective-permute-start.2 = (bf16[64,26,1]{2,0,1:T(8,128)(2,1)S(1)}, bf16[64,26,1]{2,0,1:T(8,128)(2,1)S(1)}, u32[]{:S(2)}, u32[]{:S(2)}) collective-permute-start(bf16[64,26,1]{2,0,1:T(8,128)(2,1)S(1)} %get-tuple-element.27), channel_id=1, source_target_pairs={{0,4},{4,8},{8,12},{1,5},{5,9},{9,13},{2,6},{6,10},{10,14},{3,7},{... | collective-permute-start | bytes 9992 | tf_op jit(solution)/shard_map/ppermute | solution.py:24
  42.6 5.2 %collective-permute-start.3 = (bf16[64,26,1]{2,0,1:T(8,128)(2,1)S(1)}, bf16[64,26,1]{2,0,1:T(8,128)(2,1)S(1)}, u32[]{:S(2)}, u32[]{:S(2)}) collective-permute-start(bf16[64,26,1]{2,0,1:T(8,128)(2,1)S(1)} %get-tuple-element.28), channel_id=1, source_target_pairs={{4,0},{8,4},{12,8},{5,1},{9,5},{13,9},{6,2},{10,6},{14,10},{7,3},{... | collective-permute-start | bytes 9992 | tf_op jit(solution)/shard_map/ppermute | solution.py:27
  54.0 6.7 %collective-permute-start.4 = (bf16[64,1,128]{2,0,1:T(8,128)(2,1)S(1)}, bf16[64,1,128]{2,0,1:T(8,128)(2,1)S(1)}, u32[]{:S(2)}, u32[]{:S(2)}) collective-permute-start(bf16[64,1,128]{2,0,1:T(8,128)(2,1)S(1)} %get-tuple-element.33), channel_id=1, source_target_pairs={{0,16},{1,17},{2,18},{3,19},{4,20},{5,21},{6,22},{7,23},{8,24},{9,... | collective-permute-start | bytes 49160 | tf_op jit(solution)/shard_map/ppermute | solution.py:24
  59.2 5.6 %collective-permute-start.5 = (bf16[64,1,128]{2,0,1:T(8,128)(2,1)S(1)}, bf16[64,1,128]{2,0,1:T(8,128)(2,1)S(1)}, u32[]{:S(2)}, u32[]{:S(2)}) collective-permute-start(bf16[64,1,128]{2,0,1:T(8,128)(2,1)S(1)} %get-tuple-element.34), channel_id=1, source_target_pairs={{16,0},{17,1},{18,2},{19,3},{20,4},{21,5},{22,6},{23,7},{24,8},{25... | collective-permute-start | bytes 49160 | tf_op jit(solution)/shard_map/ppermute | solution.py:27
  65.1 8.9 %collective-permute-start.6 = (bf16[64,26,1]{2,0,1:T(8,128)(2,1)S(1)}, bf16[64,26,1]{2,0,1:T(8,128)(2,1)S(1)}, u32[]{:S(2)}, u32[]{:S(2)}) collective-permute-start(bf16[64,26,1]{2,0,1:T(8,128)(2,1)S(1)} %get-tuple-element.23), channel_id=1, source_target_pairs={{0,4},{4,8},{8,12},{1,5},{5,9},{9,13},{2,6},{6,10},{10,14},{3,7},{... | collective-permute-start | bytes 9992 | tf_op jit(solution)/shard_map/ppermute | solution.py:24
  71.9 4.4 %collective-permute-start.7 = (bf16[64,26,1]{2,0,1:T(8,128)(2,1)S(1)}, bf16[64,26,1]{2,0,1:T(8,128)(2,1)S(1)}, u32[]{:S(2)}, u32[]{:S(2)}) collective-permute-start(bf16[64,26,1]{2,0,1:T(8,128)(2,1)S(1)} %get-tuple-element.24), channel_id=1, source_target_pairs={{4,0},{8,4},{12,8},{5,1},{9,5},{13,9},{6,2},{10,6},{14,10},{7,3},{... | collective-permute-start | bytes 9992 | tf_op jit(solution)/shard_map/ppermute | solution.py:27
  85.8 5.9 %copy-start.19 = (f32[9,64,64]{2,1,0:T(8,128)}, f32[9,64,64]{2,1,0:T(8,128)S(1)}, u32[]{:S(2)}) copy-start(f32[9,64,64]{2,1,0:T(8,128)S(1)} %fusion.54) | copy-start | bytes 442372
  85.8 9.9 %collective-permute-start.9 = (bf16[64,1,128]{2,0,1:T(8,128)(2,1)}, bf16[64,1,128]{2,0,1:T(8,128)(2,1)S(1)}, u32[]{:S(2)}, u32[]{:S(2)}) collective-permute-start(bf16[64,1,128]{2,0,1:T(8,128)(2,1)} %get-tuple-element.32), channel_id=1, source_target_pairs={{16,0},{17,1},{18,2},{19,3},{20,4},{21,5},{22,6},{23,7},{24,8},{25... | collective-permute-start | bytes 49160 | tf_op jit(solution)/shard_map/ppermute | solution.py:27
  87.1 8.6 %collective-permute-start.8 = (bf16[64,1,128]{2,0,1:T(8,128)(2,1)S(1)}, bf16[64,1,128]{2,0,1:T(8,128)(2,1)S(1)}, u32[]{:S(2)}, u32[]{:S(2)}) collective-permute-start(bf16[64,1,128]{2,0,1:T(8,128)(2,1)S(1)} %get-tuple-element.31), channel_id=1, source_target_pairs={{0,16},{1,17},{2,18},{3,19},{4,20},{5,21},{6,22},{7,23},{8,24},{9,... | collective-permute-start | bytes 49160 | tf_op jit(solution)/shard_map/ppermute | solution.py:24
  93.9 11.9 %copy-start.56 = (bf16[64,64,1]{1,0,2:T(8,128)(2,1)S(1)}, bf16[64,64,1]{1,0,2:T(8,128)(2,1)}, u32[]{:S(2)}) copy-start(bf16[64,64,1]{1,0,2:T(8,128)(2,1)} %reshape.222) | copy-start | bytes 24580
  95.7 10.3 %copy-start.57 = (bf16[64,64,1]{1,0,2:T(8,128)(2,1)S(1)}, bf16[64,64,1]{1,0,2:T(8,128)(2,1)}, u32[]{:S(2)}) copy-start(bf16[64,64,1]{1,0,2:T(8,128)(2,1)} %reshape.228) | copy-start | bytes 24580
  96.0 10.3 %collective-permute-start.10 = (bf16[64,26,1]{2,0,1:T(8,128)(2,1)S(1)}, bf16[64,26,1]{2,0,1:T(8,128)(2,1)S(1)}, u32[]{:S(2)}, u32[]{:S(2)}) collective-permute-start(bf16[64,26,1]{2,0,1:T(8,128)(2,1)S(1)} %get-tuple-element.19), channel_id=1, source_target_pairs={{4,0},{8,4},{12,8},{5,1},{9,5},{13,9},{6,2},{10,6},{14,10},{7,3},{... | collective-permute-start | bytes 9992 | tf_op jit(solution)/shard_map/ppermute | solution.py:27
  97.3 9.6 %collective-permute-start.11 = (bf16[64,26,1]{2,0,1:T(8,128)(2,1)S(1)}, bf16[64,26,1]{2,0,1:T(8,128)(2,1)S(1)}, u32[]{:S(2)}, u32[]{:S(2)}) collective-permute-start(bf16[64,26,1]{2,0,1:T(8,128)(2,1)S(1)} %get-tuple-element.20), channel_id=1, source_target_pairs={{0,4},{4,8},{8,12},{1,5},{5,9},{9,13},{2,6},{6,10},{10,14},{3,7},{... | collective-permute-start | bytes 9992 | tf_op jit(solution)/shard_map/ppermute | solution.py:24
  118.2 7.0 %copy-start.18 = (f32[9,64,64]{2,1,0:T(8,128)}, f32[9,64,64]{2,1,0:T(8,128)S(1)}, u32[]{:S(2)}) copy-start(f32[9,64,64]{2,1,0:T(8,128)S(1)} %fusion.61) | copy-start | bytes 442372
  118.2 9.2 %collective-permute-start.13 = (bf16[64,1,128]{2,0,1:T(8,128)(2,1)}, bf16[64,1,128]{2,0,1:T(8,128)(2,1)S(1)}, u32[]{:S(2)}, u32[]{:S(2)}) collective-permute-start(bf16[64,1,128]{2,0,1:T(8,128)(2,1)} %get-tuple-element.30), channel_id=1, source_target_pairs={{16,0},{17,1},{18,2},{19,3},{20,4},{21,5},{22,6},{23,7},{24,8},{25... | collective-permute-start | bytes 49160 | tf_op jit(solution)/shard_map/ppermute | solution.py:27
  119.5 7.9 %collective-permute-start.12 = (bf16[64,1,128]{2,0,1:T(8,128)(2,1)}, bf16[64,1,128]{2,0,1:T(8,128)(2,1)S(1)}, u32[]{:S(2)}, u32[]{:S(2)}) collective-permute-start(bf16[64,1,128]{2,0,1:T(8,128)(2,1)} %get-tuple-element.29), channel_id=1, source_target_pairs={{0,16},{1,17},{2,18},{3,19},{4,20},{5,21},{6,22},{7,23},{8,24},{9,... | collective-permute-start | bytes 49160 | tf_op jit(solution)/shard_map/ppermute | solution.py:24
  125.5 10.8 %copy-start.50 = (bf16[64,64,1]{1,0,2:T(8,128)(2,1)S(1)}, bf16[64,64,1]{1,0,2:T(8,128)(2,1)}, u32[]{:S(2)}) copy-start(bf16[64,64,1]{1,0,2:T(8,128)(2,1)} %reshape.232) | copy-start | bytes 24580
  127.5 9.2 %copy-start.51 = (bf16[64,64,1]{1,0,2:T(8,128)(2,1)S(1)}, bf16[64,64,1]{1,0,2:T(8,128)(2,1)}, u32[]{:S(2)}) copy-start(bf16[64,64,1]{1,0,2:T(8,128)(2,1)} %reshape.238) | copy-start | bytes 24580
  127.7 10.1 %collective-permute-start.14 = (bf16[64,26,1]{2,0,1:T(8,128)(2,1)S(1)}, bf16[64,26,1]{2,0,1:T(8,128)(2,1)S(1)}, u32[]{:S(2)}, u32[]{:S(2)}) collective-permute-start(bf16[64,26,1]{2,0,1:T(8,128)(2,1)S(1)} %get-tuple-element.15), channel_id=1, source_target_pairs={{4,0},{8,4},{12,8},{5,1},{9,5},{13,9},{6,2},{10,6},{14,10},{7,3},{... | collective-permute-start | bytes 9992 | tf_op jit(solution)/shard_map/ppermute | solution.py:27
  129.0 8.8 %collective-permute-start.15 = (bf16[64,26,1]{2,0,1:T(8,128)(2,1)S(1)}, bf16[64,26,1]{2,0,1:T(8,128)(2,1)S(1)}, u32[]{:S(2)}, u32[]{:S(2)}) collective-permute-start(bf16[64,26,1]{2,0,1:T(8,128)(2,1)S(1)} %get-tuple-element.16), channel_id=1, source_target_pairs={{0,4},{4,8},{8,12},{1,5},{5,9},{9,13},{2,6},{6,10},{10,14},{3,7},{... | collective-permute-start | bytes 9992 | tf_op jit(solution)/shard_map/ppermute | solution.py:24
  145.5 135.7 %copy-start.25 = (f32[4416]{0:T(1024)S(1)}, f32[4416]{0:T(1024)}, u32[]{:S(2)}) copy-start(f32[4416]{0:T(1024)} %param.7) | copy-start | bytes 52996
  145.5 179.9 %copy-start.17 = (f32[141312]{0:T(1024)S(1)}, f32[141312]{0:T(1024)}, u32[]{:S(2)}) copy-start(f32[141312]{0:T(1024)} %param.6) | copy-start | bytes 1695748
  (32 other events, 51.3 us)
Sparse Core Ops, SparseCore 0:
  146.9 134.3 all-reduce.2
where the time goes:
time: 336 us; the launch traced here: 335 us
  waiting for transfers between devices  143 us (43%)
  starting transfers between devices  54.4 us (16%)
  blocking collectives  41.4 us (12%)
  matrix products  36.9 us (11%)
  local copies, waits for them, and re-layouts  30.4 us (9%)
  between operations  17.9 us (5%)
  other arithmetic  10.6 us (3%)
    psum x1, waiting for transfers between devices, local(): total = lax.psum(flat, ('row', 'col', 'dp'))  135 us
    ppermute x8, starting transfers between devices, extended(): lax.ppermute(lax.slice_in_dim(block, block.shape[dim] - width, None, axis...  43.8 us
    psum x1, blocking collectives, local(): lax.psum((jnp.sum(jnp.abs(mixed)), loss_part), ('row', 'col', 'dp'))  41.4 us
    ppermute x8, starting transfers between devices, extended(): lax.ppermute(lax.slice_in_dim(block, 0, width, axis=dim), axis, backward)  10.5 us
    squeeze x32, local copies, waits for them, and re-layouts, conv_taps(): w_mid[position]  10.4 us
    dot_general x17, matrix products, local(): jnp.einsum('io,ohw->ihw', w_mid[position], spread_back[:, shift_row:shift...  10.4 us
    dot_general x18, matrix products, conv_taps(): jnp.einsum('io,ihw->ohw', w_mid[position], padded[:, shift_row:shift_row...  9.34 us
    unnamed x133, local copies, waits for them, and re-layouts  8.18 us
  transfers between devices with their start and end apart: 17, of which 5 were waited for; matrix products, arithmetic and copies ran while one was open for 9% of the time, Pallas kernels for 0%

commit v1 on v0

--- a/solution.py
+++ b/solution.py
@@ -1,6 +1,8 @@
 import jax
 import jax.numpy as jnp
 from jax import lax
+from jax.experimental import pallas as pl
+from jax.experimental.pallas import tpu as pltpu
 from jax.sharding import PartitionSpec as P
 
 C = 256
@@ -66,6 +68,173 @@
             preferred_element_type=jnp.float32,
         )
     return total
+
+
+MESH_ID = pl.DeviceIdType.MESH
+AXES = ("row", "col", "dp")
+
+
+def share_rows(share, count):
+    first = [d * share // 128 for d in range(count)]
+    last = [-(-(d + 1) * share // 128) for d in range(count)]
+    return max(b - a for a, b in zip(first, last))
+
+
+def split_col(ncol):
+    return 2 if ncol % 2 == 0 else 1
+
+
+def peers(sizes):
+    nrow, ncol, ndp = sizes
+    row, col, dp = (lax.axis_index(a) for a in AXES)
+
+    def plane(k):
+        place = lax.rem(row * ncol + col + k, nrow * ncol)
+        return (place // ncol, lax.rem(place, ncol), dp)
+
+    def line(k):
+        return (row, col, lax.rem(dp + k, ndp))
+
+    return plane, line
+
+
+def greet(sizes):
+    nrow, ncol, ndp = sizes
+    plane, line = peers(sizes)
+    barrier = pltpu.get_barrier_semaphore()
+    for target, count in ((plane, nrow * ncol), (line, ndp)):
+        def one(k, carry, target=target):
+            pl.semaphore_signal(barrier, inc=1, device_id=target(k), device_id_type=MESH_ID)
+            return carry
+        lax.fori_loop(1, count, one, 0)
+    pl.semaphore_wait(barrier, nrow * ncol - 1 + ndp - 1)
+
+
+def exchange(count, source, landing, target, send, recv):
+    def copy(k):
+        return pltpu.make_async_remote_copy(
+            src_ref=source(k), dst_ref=landing.at[k - 1], send_sem=send.at[k - 1],
+            recv_sem=recv.at[k - 1], device_id=target(k), device_id_type=MESH_ID)
+
+    def start(k, carry):
+        copy(k).start()
+        return carry
+
+    def finish(k, carry):
+        copy(k).wait()
+        return carry
+
+    lax.fori_loop(1, count, start, 0)
+    lax.fori_loop(1, count, finish, 0)
+
+
+def lion_kernel(sizes, share, params, flat_ref, loss_ref, mom_ref, wgt_ref, out_ref, total_ref,
+                held, a1, r1, a2, r2, a3, r3, r4, mine, rp, line_sum, rl, *sems):
+    nrow, ncol, ndp = sizes
+    lo_n = split_col(ncol)
+    hi_n = ncol // lo_n
+    rows = mom_ref.shape[0]
+    row, col, dp = (lax.axis_index(a) for a in AXES)
+    lo, hi = lax.rem(col, lo_n), col // lo_n
+    greet(sizes)
+    for r in range(nrow):
+        for c in range(ncol):
+            for z in range(ndp):
+                start = ((r * ncol + c) * ndp + z) * share // 128
+                have = min(rows, flat_ref.shape[0] - start)
+                held[c % lo_n, r, c // lo_n, z, 0:have] = flat_ref[start : start + have, :]
+
+    def step(count, me, now, landing, later, where, send, recv):
+        exchange(count, lambda k: now.at[lax.rem(me + k, count)], landing,
+                 lambda k: where(lax.rem(me + k, count)), send, recv)
+        total = now[me]
+        for k in range(count - 1):
+            total = total + landing[k]
+        if later is None:
+            return total
+        later[...] = total
+
+    step(lo_n, lo, held, r1, a1, lambda p: (row, hi * lo_n + p, dp), sems[0], sems[1])
+    step(nrow, row, a1, r2, a2, lambda p: (p, col, dp), sems[2], sems[3])
+    step(hi_n, hi, a2, r3, a3, lambda p: (row, p * lo_n + lo, dp), sems[4], sems[5])
+    grad = step(ndp, dp, a3, r4, None, lambda p: (row, col, p), sems[6], sems[7])
+
+    me = (row * ncol + col) * ndp + dp
+    skip = lax.rem(me * share, 128)
+    place = (lax.broadcasted_iota(jnp.int32, (rows, 128), 0) * 128
+             + lax.broadcasted_iota(jnp.int32, (rows, 128), 1))
+    inside = jnp.logical_and(place >= skip, place < skip + share)
+    momentum = mom_ref[...]
+    weight = wgt_ref[...]
+    mixed = beta_one * momentum + (1.0 - beta_one) * grad
+    size = jnp.abs(mixed)
+    part = jnp.sum(jnp.where(inside, size, 0.0), axis=0, keepdims=True)
+    which = lax.broadcasted_iota(jnp.int32, (8, 128), 0)
+    mine[...] = jnp.where(which == 0, part, jnp.where(which == 1, loss_ref[...], 0.0))
+    plane, line = peers(sizes)
+    exchange(nrow * ncol, lambda k: mine, rp, plane, sems[8], sems[9])
+    total = mine[...]
+    for k in range(nrow * ncol - 1):
+        total = total + rp[k]
+    line_sum[...] = total
+    exchange(ndp, lambda k: line_sum, rl, line, sems[10], sems[11])
+    for k in range(ndp - 1):
+        total = total + rl[k]
+    total_ref[...] = jnp.broadcast_to(jnp.sum(total, axis=1, keepdims=True), (8, 128))
+    tau = jnp.sum(total[0:1, :], axis=1, keepdims=True) / params + 1e-06
+    update = mixed / (size + tau)
+    out_ref[0] = weight - learn_rate * (update + weight_decay * weight)
+    out_ref[1] = beta_two * momentum + (1.0 - beta_two) * grad
+    out_ref[2] = update
+
+
+def lion_step(flat, loss_part, weights, momentum):
+    sizes = tuple(lax.axis_size(a) for a in AXES)
+    nrow, ncol, ndp = sizes
+    count = nrow * ncol * ndp
+    share = momentum.shape[0]
+    params = weights.shape[0]
+    rows = share_rows(share, count)
+    me = lax.axis_index(AXES)
+    skip = me * share % 128
+    first = me * share // 128
+    mom = lax.dynamic_update_slice(jnp.zeros((rows * 128,), jnp.float32), momentum, (skip,))
+    spare = max(0, (count - 1) * share // 128 + rows - params // 128)
+    wgt = jnp.pad(weights.reshape(-1, 128), ((0, spare), (0, 0)))
+    wgt = lax.dynamic_slice_in_dim(wgt, first, rows, 0)
+    lane0 = jnp.arange(128)[None, :] == 0
+    loss_row = jnp.where(lane0, loss_part, 0.0)
+    lo_n = split_col(ncol)
+    hi_n = ncol // lo_n
+    f32 = jnp.float32
+    tail = (rows, 128)
+    plane_n = nrow * ncol
+    counts = (lo_n, nrow, hi_n, ndp, plane_n, ndp)
+    sems = [pltpu.SemaphoreType.DMA((max(n - 1, 1),)) for n in counts for _ in range(2)]
+    vmem = pl.BlockSpec(memory_space=pltpu.VMEM)
+
+    def land(n, *rest):
+        return pltpu.VMEM((max(n - 1, 1),) + rest + tail, f32)
+
+    out, total = pl.pallas_call(
+        lambda *refs: lion_kernel(sizes, share, params, *refs),
+        out_shape=(jax.ShapeDtypeStruct((3,) + tail, f32), jax.ShapeDtypeStruct((8, 128), f32)),
+        in_specs=[vmem] * 4,
+        out_specs=(vmem, vmem),
+        scratch_shapes=[
+            pltpu.VMEM((lo_n, nrow, hi_n, ndp) + tail, f32),
+            pltpu.VMEM((nrow, hi_n, ndp) + tail, f32), land(lo_n, nrow, hi_n, ndp),
+            pltpu.VMEM((hi_n, ndp) + tail, f32), land(nrow, hi_n, ndp),
+            pltpu.VMEM((ndp,) + tail, f32), land(hi_n, ndp),
+            land(ndp),
+            pltpu.VMEM((8, 128), f32), pltpu.VMEM((max(plane_n - 1, 1), 8, 128), f32),
+            pltpu.VMEM((8, 128), f32), pltpu.VMEM((max(ndp - 1, 1), 8, 128), f32),
+        ] + sems,
+        compiler_params=pltpu.CompilerParams(
+            collective_id=0, has_side_effects=True, vmem_limit_bytes=40 * 1024 * 1024),
+    )(flat.reshape(-1, 128), loss_row, mom.reshape(rows, 128), wgt)
+    out = lax.dynamic_slice_in_dim(out.reshape(3, rows * 128), skip, share, 1)
+    return out[0], out[1], out[2], total[1, 0]
 
 
 def local(image, labels, weights, momentum):
@@ -160,17 +329,7 @@
             ).astype(jnp.bfloat16)
         grads[number] = jnp.concatenate([grad_in.ravel(), grad_mid.ravel(), grad_out.ravel()])
     flat = jnp.concatenate([grads[0], grads[1], grad_head.ravel()])
-    share = momentum.shape[0]
-    start = lax.axis_index(("row", "col", "dp")) * share
-    total = lax.psum(flat, ("row", "col", "dp"))
-    grad = lax.dynamic_slice_in_dim(total, start, share, 0)
-    weight_share = lax.dynamic_slice_in_dim(weights, start, share, 0)
-    mixed = beta_one * momentum + (1.0 - beta_one) * grad
-    abs_total, loss_total = lax.psum((jnp.sum(jnp.abs(mixed)), loss_part), ("row", "col", "dp"))
-    scale_tau = abs_total / weights.shape[0] + 1e-06
-    update = mixed / (jnp.abs(mixed) + scale_tau)
-    new_weights = weight_share - learn_rate * (update + weight_decay * weight_share)
-    new_momentum = beta_two * momentum + (1.0 - beta_two) * grad
+    new_weights, new_momentum, update, loss_total = lion_step(flat, loss_part, weights, momentum)
     return (new_weights, new_momentum, update, loss_total / total_tiles)
 
 

time: 336 us -> 183 us (0.54)
  waiting for transfers between devices: 143 us -> 9.47 us
  blocking collectives: 41.4 us -> 0 us
  Pallas kernels: 0 us -> 32.3 us
  between operations: 17.9 us -> 3.87 us
  local copies, waits for them, and re-layouts: 30.4 us -> 37.1 us
    psum x1 -> x0, waiting for transfers between devices: 135 us -> none  [local(): total = lax.psum(flat, ('row', 'col', 'dp'))]
    psum x1 -> x0, blocking collectives: 41.4 us -> none  [local(): lax.psum((jnp.sum(jnp.abs(mixed)), loss_part), ('row', 'col', 'dp'))]
    pallas_call x0 -> x1, Pallas kernels: none -> 32.3 us  [lion_step(): pl.pallas_call(lambda *refs: lion_kernel(sizes, share, params, *refs), ou...]
    unnamed x133 -> x138, local copies, waits for them, and re-layouts: 8.18 us -> 8.67 us
  transfers between devices with their start and end apart: 17 -> 16, of which waited for: 5 -> 4; matrix products, arithmetic and copies ran while one was open for 9% -> 20% of each run, Pallas kernels for 0% -> 0%
where the time goes in v1:
time: 183 us; the launch traced here: 181 us
  starting transfers between devices  53.8 us (29%)
  local copies, waits for them, and re-layouts  37.1 us (20%)
  matrix products  36.2 us (20%)
  Pallas kernels  32.3 us (18%)
  waiting for transfers between devices  9.47 us (5%)
  other arithmetic  8.32 us (5%)
  between operations  3.87 us (2%)
    ppermute x8, starting transfers between devices, extended(): lax.ppermute(lax.slice_in_dim(block, block.shape[dim] - width, None, axis...  43.3 us
    pallas_call x1, Pallas kernels, lion_step(): pl.pallas_call(lambda *refs: lion_kernel(sizes, share, params, *refs), ou...  32.3 us
    squeeze x32, local copies, waits for them, and re-layouts, conv_taps(): w_mid[position]  12.9 us
    ppermute x8, starting transfers between devices, extended(): lax.ppermute(lax.slice_in_dim(block, 0, width, axis=dim), axis, backward)  10.5 us
    dot_general x17, matrix products, local(): jnp.einsum('io,ohw->ihw', w_mid[position], spread_back[:, shift_row:shift...  10.4 us
    ppermute x8, waiting for transfers between devices, extended(): lax.ppermute(lax.slice_in_dim(block, 0, width, axis=dim), axis, backward)  8.85 us
    unnamed x138, local copies, waits for them, and re-layouts  8.67 us
    dot_general x18, matrix products, conv_taps(): jnp.einsum('io,ihw->ohw', w_mid[position], padded[:, shift_row:shift_row...  8.64 us
  transfers between devices with their start and end apart: 16, of which 4 were waited for; matrix products, arithmetic and copies ran while one was open for 20% of the time, Pallas kernels for 0%

profile of v1, /device:TPU:0, one launch (start us, length us, event | category | flops | bytes accessed | tf_op | source)
XLA Modules:
  0.0 181.1 jit_solution(12786468914150625617)
XLA Ops:
  0.6 1.1 convert.8
  3.8 2.1 %copy.93 = bf16[256,24,128]{0,2,1:T(8,128)(2,1)S(1)} copy(bf16[256,24,128]{2,1,0:T(8,128)(2,1)} %bitcast.302) | data formatting | bytes 3145728 | tf_op jit(solution)/shard_map/squeeze | solution.py:241
  6.0 2.3 %convert_reduce_fusion.1 = (u32[64,128]{1,0:T(8,128)}, bf16[64,24,128]{2,0,1:T(8,128)(2,1)S(1)}) fusion(bf16[256,24,128]{0,2,1:T(8,128)(2,1)S(1)} %copy.93, bf16[256,64]{1,0:T(8,128)(2,1)} %convert_element_type.87), kind=kOutput, calls=%fused_computation.119 | convolution fusion | flops 102227968 | bytes 2031616 | tf_op jit(solution)/shard_map/io,ihw->ohw/dot_general | solution.py:255
  8.9 5.5 %collective-permute-start = (bf16[64,1,128]{2,0,1:T(8,128)(2,1)}, bf16[64,1,128]{2,0,1:T(8,128)(2,1)}, u32[]{:S(2)}, u32[]{:S(2)}) collective-permute-start(bf16[64,1,128]{2,0,1:T(8,128)(2,1)} %get-tuple-element.37), channel_id=1, source_target_pairs={{0,16},{1,17},{2,18},{3,19},{4,20},{5,21},{6,22},{7,23},{8,24},{9,... | collective-permute-start | bytes 49160 | tf_op jit(solution)/shard_map/ppermute | solution.py:26
  14.3 1.3 collective-permute-start.1
  16.3 1.4 squeeze.91
  17.7 1.9 %fusion.157 = f32[24,128,64]{1,2,0:T(8,128)} fusion(bf16[64,24,128]{2,0,1:T(8,128)(2,1)S(1)} %get-tuple-element.62, bf16[64,64]{1,0:T(8,128)(2,1)} %squeeze.91), kind=kOutput, calls=%fused_computation.224 | convolution fusion | flops 25165824 | bytes 1187840 | tf_op jit(solution)/shard_map/io,ihw->ohw/dot_general | solution.py:64
  19.6 1.6 and_convert_fusion
  21.2 0.7 constant_dynamic-slice_fusion.refs_3_
  22.2 1.9 %copy.59 = bf16[1,256,24,128]{1,3,2,0:T(8,128)(2,1)} copy(bf16[1,256,24,128]{3,2,1,0:T(8,128)(2,1)S(1)} %copy-done.2) | data formatting | bytes 3145728 | tf_op args[0]
  38.5 0.8 pad_maximum_fusion.4
  39.5 1.5 collective-permute-start.2
  41.0 1.3 collective-permute-start.3
  42.3 1.0 fusion.139
  43.7 2.5 %collective-permute-done.3 = bf16[64,26,1]{2,0,1:T(8,128)(2,1)S(1)} collective-permute-done((bf16[64,26,1]{2,0,1:T(8,128)(2,1)S(1)}, bf16[64,26,1]{2,0,1:T(8,128)(2,1)S(1)}, u32[]{:S(2)}, u32[]{:S(2)}) %collective-permute-start.3) | collective-permute-done | bytes 3360 | tf_op jit(solution)/shard_map/ppermute | solution.py:29
  46.2 1.3 maximum_maximum_fusion
  50.2 0.9 copy-done.3
  52.4 4.5 %collective-permute-start.4 = (bf16[64,1,128]{2,0,1:T(8,128)(2,1)S(1)}, bf16[64,1,128]{2,0,1:T(8,128)(2,1)S(1)}, u32[]{:S(2)}, u32[]{:S(2)}) collective-permute-start(bf16[64,1,128]{2,0,1:T(8,128)(2,1)S(1)} %get-tuple-element.35), channel_id=1, source_target_pairs={{0,16},{1,17},{2,18},{3,19},{4,20},{5,21},{6,22},{7,23},{8,24},{9,... | collective-permute-start | bytes 49160 | tf_op jit(solution)/shard_map/ppermute | solution.py:26
  56.9 1.3 collective-permute-start.5
  58.6 4.0 %collective-permute-done.5 = bf16[64,1,128]{2,0,1:T(8,128)(2,1)S(1)} collective-permute-done((bf16[64,1,128]{2,0,1:T(8,128)(2,1)S(1)}, bf16[64,1,128]{2,0,1:T(8,128)(2,1)S(1)}, u32[]{:S(2)}, u32[]{:S(2)}) %collective-permute-start.5) | collective-permute-done | bytes 16416 | tf_op jit(solution)/shard_map/ppermute | solution.py:29
  62.9 6.8 %collective-permute-start.6 = (bf16[64,26,1]{2,0,1:T(8,128)(2,1)S(1)}, bf16[64,26,1]{2,0,1:T(8,128)(2,1)S(1)}, u32[]{:S(2)}, u32[]{:S(2)}) collective-permute-start(bf16[64,26,1]{2,0,1:T(8,128)(2,1)S(1)} %get-tuple-element.25), channel_id=1, source_target_pairs={{0,4},{4,8},{8,12},{1,5},{5,9},{9,13},{2,6},{6,10},{10,14},{3,7},{... | collective-permute-start | bytes 9992 | tf_op jit(solution)/shard_map/ppermute | solution.py:26
  69.7 1.5 collective-permute-start.7
  71.8 2.3 %collective-permute-done.7 = bf16[64,26,1]{2,0,1:T(8,128)(2,1)S(1)} collective-permute-done((bf16[64,26,1]{2,0,1:T(8,128)(2,1)S(1)}, bf16[64,26,1]{2,0,1:T(8,128)(2,1)S(1)}, u32[]{:S(2)}, u32[]{:S(2)}) %collective-permute-start.7) | collective-permute-done | bytes 3360 | tf_op jit(solution)/shard_map/ppermute | solution.py:29
  77.0 0.8 convert_reduce_fusion
  79.6 1.0 convolution_bitcast_fusion.3
  84.4 1.3 collective-permute-start.9
  85.7 4.5 %collective-permute-start.8 = (bf16[64,1,128]{2,0,1:T(8,128)(2,1)}, bf16[64,1,128]{2,0,1:T(8,128)(2,1)S(1)}, u32[]{:S(2)}, u32[]{:S(2)}) collective-permute-start(bf16[64,1,128]{2,0,1:T(8,128)(2,1)} %get-tuple-element.33), channel_id=1, source_target_pairs={{0,16},{1,17},{2,18},{3,19},{4,20},{5,21},{6,22},{7,23},{8,24},{9,... | collective-permute-start | bytes 49160 | tf_op jit(solution)/shard_map/ppermute | solution.py:26
  90.2 1.2 fusion.197
  92.1 0.7 reshape.224
  92.8 1.5 copy.150
  94.3 1.1 reshape.222
  95.7 1.3 collective-permute-start.10
  97.0 8.5 %collective-permute-start.11 = (bf16[64,26,1]{2,0,1:T(8,128)(2,1)S(1)}, bf16[64,26,1]{2,0,1:T(8,128)(2,1)S(1)}, u32[]{:S(2)}, u32[]{:S(2)}) collective-permute-start(bf16[64,26,1]{2,0,1:T(8,128)(2,1)S(1)} %get-tuple-element.22), channel_id=1, source_target_pairs={{0,4},{4,8},{8,12},{1,5},{5,9},{9,13},{2,6},{6,10},{10,14},{3,7},{... | collective-permute-start | bytes 9992 | tf_op jit(solution)/shard_map/ppermute | solution.py:26
  109.9 1.0 copy-done.12
  114.2 1.0 fusion.53
  117.2 1.3 collective-permute-start.13
  118.5 4.5 %collective-permute-start.12 = (bf16[64,1,128]{2,0,1:T(8,128)(2,1)}, bf16[64,1,128]{2,0,1:T(8,128)(2,1)S(1)}, u32[]{:S(2)}, u32[]{:S(2)}) collective-permute-start(bf16[64,1,128]{2,0,1:T(8,128)(2,1)} %get-tuple-element.31), channel_id=1, source_target_pairs={{0,16},{1,17},{2,18},{3,19},{4,20},{5,21},{6,22},{7,23},{8,24},{9,... | collective-permute-start | bytes 49160 | tf_op jit(solution)/shard_map/ppermute | solution.py:26
  123.1 1.1 fusion.198
  124.6 1.1 reshape.219
  127.3 1.3 collective-permute-start.14
  128.6 7.4 %collective-permute-start.15 = (bf16[64,26,1]{2,0,1:T(8,128)(2,1)S(1)}, bf16[64,26,1]{2,0,1:T(8,128)(2,1)S(1)}, u32[]{:S(2)}, u32[]{:S(2)}) collective-permute-start(bf16[64,26,1]{2,0,1:T(8,128)(2,1)S(1)} %get-tuple-element.18), channel_id=1, source_target_pairs={{0,4},{4,8},{8,12},{1,5},{5,9},{9,13},{2,6},{6,10},{10,14},{3,7},{... | collective-permute-start | bytes 9992 | tf_op jit(solution)/shard_map/ppermute | solution.py:26
  136.3 1.1 fusion.76
  138.5 1.2 fusion.78
  140.0 1.1 fusion.74
  141.2 1.3 fusion.13
  142.7 2.5 %fusion.49 = f32[256,64]{0,1:T(8,128)S(1)} fusion(bf16[256,24,128]{0,2,1:T(8,128)(2,1)S(1)} %copy-done.1, pred[64,24,128]{2,0,1:T(32,128)(4,1)S(1)} %copy-done.15, f32[24,128,64]{1,2,0:T(8,128)} %fusion.74, f32[24,128,64]{1,2,0:T(8,128)} %fusion.76, f32[24,128,64]{1,2,0:T(8,128)} %fusion.78, f32[24,128,64]{1,2,0:T(8,128)} %fusion.13, ...), kind=kOutput, calls=%fused_computation.68 | convolution fusion | flops 127008768 | bytes 5390336 | tf_op jit(solution)/shard_map/ihw,ohw->io/dot_general | solution.py:324
  145.6 32.3 %shard_map.75 = (f32[3,35,128]{2,1,0:T(8,128)S(1)}, f32[8,128]{1,0:T(8,128)S(1)}) custom-call(f32[1104,128]{1,0:T(8,128)S(1)} %bitcast.299, f32[1,128]{1,0:T(1,128)S(1)} %compare_select_fusion.4.refs_1_, f32[35,128]{1,0:T(8,128)S(1)} %bitcast.300, f32[35,128]{1,0:T(8,128)S(1)} %constant_dynamic-slice_fusion.refs_3_), custom_call_target="tpu_custom_call" | custom-call | tf_op jit(solution)/shard_map/pallas_call | solution.py:219
  179.1 0.8 dynamic-slice_reduce_fusion
  (270 shorter events, 46.6 us)
Async XLA Ops:
  5.9 13.7 %copy-start = (bf16[256,24,128]{0,2,1:T(8,128)(2,1)}, bf16[256,24,128]{0,2,1:T(8,128)(2,1)S(1)}, u32[]{:S(2)}) copy-start(bf16[256,24,128]{0,2,1:T(8,128)(2,1)S(1)} %copy.93) | copy-start | bytes 4718596
  5.9 9.7 %copy-start.14 = (bf16[141312]{0:T(1024)(128)(2,1)S(1)}, bf16[141312]{0:T(1024)(128)(2,1)}, u32[]{:S(2)}) copy-start(bf16[141312]{0:T(1024)(128)(2,1)} %copy-done.13) | copy-start | bytes 847876
  6.0 16.0 %copy-start.2 = (bf16[1,256,24,128]{3,2,1,0:T(8,128)(2,1)S(1)}, bf16[1,256,24,128]{3,2,1,0:T(8,128)(2,1)}, u32[]{:S(2)}) copy-start(bf16[1,256,24,128]{3,2,1,0:T(8,128)(2,1)} %param.4) | copy-start | bytes 4718596
  8.9 29.7 %collective-permute-start = (bf16[64,1,128]{2,0,1:T(8,128)(2,1)}, bf16[64,1,128]{2,0,1:T(8,128)(2,1)}, u32[]{:S(2)}, u32[]{:S(2)}) collective-permute-start(bf16[64,1,128]{2,0,1:T(8,128)(2,1)} %get-tuple-element.37), channel_id=1, source_target_pairs={{0,16},{1,17},{2,18},{3,19},{4,20},{5,21},{6,22},{7,23},{8,24},{9,... | collective-permute-start | bytes 49160 | tf_op jit(solution)/shard_map/ppermute | solution.py:26
  14.3 24.2 %collective-permute-start.1 = (bf16[64,1,128]{2,0,1:T(8,128)(2,1)}, bf16[64,1,128]{2,0,1:T(8,128)(2,1)S(1)}, u32[]{:S(2)}, u32[]{:S(2)}) collective-permute-start(bf16[64,1,128]{2,0,1:T(8,128)(2,1)} %get-tuple-element.38), channel_id=1, source_target_pairs={{16,0},{17,1},{18,2},{19,3},{20,4},{21,5},{22,6},{23,7},{24,8},{25... | collective-permute-start | bytes 49160 | tf_op jit(solution)/shard_map/ppermute | solution.py:29
  22.0 3.5 %copy-start.40 = (bf16[4096]{0:T(1024)(128)(2,1)S(1)}, bf16[4096]{0:T(1024)(128)(2,1)}, u32[]{:S(2)}) copy-start(bf16[4096]{0:T(1024)(128)(2,1)} %get-tuple-element.44) | copy-start | bytes 24580
  22.0 4.3 %copy-start.39 = (bf16[4096]{0:T(1024)(128)(2,1)S(1)}, bf16[4096]{0:T(1024)(128)(2,1)}, u32[]{:S(2)}) copy-start(bf16[4096]{0:T(1024)(128)(2,1)} %get-tuple-element.45) | copy-start | bytes 24580
  22.0 5.1 %copy-start.38 = (bf16[4096]{0:T(1024)(128)(2,1)S(1)}, bf16[4096]{0:T(1024)(128)(2,1)}, u32[]{:S(2)}) copy-start(bf16[4096]{0:T(1024)(128)(2,1)} %get-tuple-element.43) | copy-start | bytes 24580
  22.0 5.2 %copy-start.37 = (bf16[4096]{0:T(1024)(128)(2,1)S(1)}, bf16[4096]{0:T(1024)(128)(2,1)}, u32[]{:S(2)}) copy-start(bf16[4096]{0:T(1024)(128)(2,1)} %get-tuple-element.47) | copy-start | bytes 24580
  22.0 6.0 %copy-start.36 = (bf16[4096]{0:T(1024)(128)(2,1)S(1)}, bf16[4096]{0:T(1024)(128)(2,1)}, u32[]{:S(2)}) copy-start(bf16[4096]{0:T(1024)(128)(2,1)} %get-tuple-element.41) | copy-start | bytes 24580
  22.0 6.7 %copy-start.35 = (bf16[4096]{0:T(1024)(128)(2,1)S(1)}, bf16[4096]{0:T(1024)(128)(2,1)}, u32[]{:S(2)}) copy-start(bf16[4096]{0:T(1024)(128)(2,1)} %get-tuple-element.42) | copy-start | bytes 24580
  22.0 7.5 %copy-start.34 = (bf16[4096]{0:T(1024)(128)(2,1)S(1)}, bf16[4096]{0:T(1024)(128)(2,1)}, u32[]{:S(2)}) copy-start(bf16[4096]{0:T(1024)(128)(2,1)} %get-tuple-element.40) | copy-start | bytes 24580
  22.0 8.2 %copy-start.33 = (bf16[4096]{0:T(1024)(128)(2,1)S(1)}, bf16[4096]{0:T(1024)(128)(2,1)}, u32[]{:S(2)}) copy-start(bf16[4096]{0:T(1024)(128)(2,1)} %get-tuple-element.39) | copy-start | bytes 24580
  22.1 9.0 %copy-start.32 = (bf16[4096]{0:T(1024)(128)(2,1)S(1)}, bf16[4096]{0:T(1024)(128)(2,1)}, u32[]{:S(2)}) copy-start(bf16[4096]{0:T(1024)(128)(2,1)} %get-tuple-element.55) | copy-start | bytes 24580
  22.1 9.7 %copy-start.31 = (bf16[4096]{0:T(1024)(128)(2,1)S(1)}, bf16[4096]{0:T(1024)(128)(2,1)}, u32[]{:S(2)}) copy-start(bf16[4096]{0:T(1024)(128)(2,1)} %get-tuple-element.53) | copy-start | bytes 24580
  22.1 10.5 %copy-start.30 = (bf16[4096]{0:T(1024)(128)(2,1)S(1)}, bf16[4096]{0:T(1024)(128)(2,1)}, u32[]{:S(2)}) copy-start(bf16[4096]{0:T(1024)(128)(2,1)} %get-tuple-element.54) | copy-start | bytes 24580
  22.1 11.3 %copy-start.29 = (bf16[4096]{0:T(1024)(128)(2,1)S(1)}, bf16[4096]{0:T(1024)(128)(2,1)}, u32[]{:S(2)}) copy-start(bf16[4096]{0:T(1024)(128)(2,1)} %get-tuple-element.52) | copy-start | bytes 24580
  22.1 11.9 %copy-start.28 = (bf16[4096]{0:T(1024)(128)(2,1)S(1)}, bf16[4096]{0:T(1024)(128)(2,1)}, u32[]{:S(2)}) copy-start(bf16[4096]{0:T(1024)(128)(2,1)} %get-tuple-element.56) | copy-start | bytes 24580
  22.1 12.7 %copy-start.27 = (bf16[4096]{0:T(1024)(128)(2,1)S(1)}, bf16[4096]{0:T(1024)(128)(2,1)}, u32[]{:S(2)}) copy-start(bf16[4096]{0:T(1024)(128)(2,1)} %get-tuple-element.49) | copy-start | bytes 24580
  22.1 13.4 %copy-start.26 = (bf16[4096]{0:T(1024)(128)(2,1)S(1)}, bf16[4096]{0:T(1024)(128)(2,1)}, u32[]{:S(2)}) copy-start(bf16[4096]{0:T(1024)(128)(2,1)} %get-tuple-element.50) | copy-start | bytes 24580
  22.1 14.2 %copy-start.25 = (bf16[4096]{0:T(1024)(128)(2,1)S(1)}, bf16[4096]{0:T(1024)(128)(2,1)}, u32[]{:S(2)}) copy-start(bf16[4096]{0:T(1024)(128)(2,1)} %get-tuple-element.48) | copy-start | bytes 24580
  22.1 15.0 %copy-start.24 = (bf16[4096]{0:T(1024)(128)(2,1)S(1)}, bf16[4096]{0:T(1024)(128)(2,1)}, u32[]{:S(2)}) copy-start(bf16[4096]{0:T(1024)(128)(2,1)} %get-tuple-element.51) | copy-start | bytes 24580
  22.1 15.7 %copy-start.23 = (bf16[16384]{0:T(1024)(128)(2,1)S(1)}, bf16[16384]{0:T(1024)(128)(2,1)}, u32[]{:S(2)}) copy-start(bf16[16384]{0:T(1024)(128)(2,1)} %get-tuple-element.59) | copy-start | bytes 98308
  22.2 15.7 %copy-start.21 = (bf16[16384]{0:T(1024)(128)(2,1)S(1)}, bf16[16384]{0:T(1024)(128)(2,1)}, u32[]{:S(2)}) copy-start(bf16[16384]{0:T(1024)(128)(2,1)} %get-tuple-element.57) | copy-start | bytes 98308
  22.2 15.8 %copy-start.22 = (bf16[16384]{0:T(1024)(128)(2,1)S(1)}, bf16[16384]{0:T(1024)(128)(2,1)}, u32[]{:S(2)}) copy-start(bf16[16384]{0:T(1024)(128)(2,1)} %get-tuple-element.58) | copy-start | bytes 98308
  22.2 16.0 %copy-start.62 = (f32[4416]{0:T(1024)S(1)}, f32[4416]{0:T(1024)}, u32[]{:S(2)}) copy-start(f32[4416]{0:T(1024)} %param.7) | copy-start | bytes 52996
  39.5 4.1 %collective-permute-start.2 = (bf16[64,26,1]{2,0,1:T(8,128)(2,1)S(1)}, bf16[64,26,1]{2,0,1:T(8,128)(2,1)S(1)}, u32[]{:S(2)}, u32[]{:S(2)}) collective-permute-start(bf16[64,26,1]{2,0,1:T(8,128)(2,1)S(1)} %get-tuple-element.29), channel_id=1, source_target_pairs={{0,4},{4,8},{8,12},{1,5},{5,9},{9,13},{2,6},{6,10},{10,14},{3,7},{... | collective-permute-start | bytes 9992 | tf_op jit(solution)/shard_map/ppermute | solution.py:26
  41.0 5.2 %collective-permute-start.3 = (bf16[64,26,1]{2,0,1:T(8,128)(2,1)S(1)}, bf16[64,26,1]{2,0,1:T(8,128)(2,1)S(1)}, u32[]{:S(2)}, u32[]{:S(2)}) collective-permute-start(bf16[64,26,1]{2,0,1:T(8,128)(2,1)S(1)} %get-tuple-element.30), channel_id=1, source_target_pairs={{4,0},{8,4},{12,8},{5,1},{9,5},{13,9},{6,2},{10,6},{14,10},{7,3},{... | collective-permute-start | bytes 9992 | tf_op jit(solution)/shard_map/ppermute | solution.py:29
  52.4 6.2 %collective-permute-start.4 = (bf16[64,1,128]{2,0,1:T(8,128)(2,1)S(1)}, bf16[64,1,128]{2,0,1:T(8,128)(2,1)S(1)}, u32[]{:S(2)}, u32[]{:S(2)}) collective-permute-start(bf16[64,1,128]{2,0,1:T(8,128)(2,1)S(1)} %get-tuple-element.35), channel_id=1, source_target_pairs={{0,16},{1,17},{2,18},{3,19},{4,20},{5,21},{6,22},{7,23},{8,24},{9,... | collective-permute-start | bytes 49160 | tf_op jit(solution)/shard_map/ppermute | solution.py:26
  56.9 5.6 %collective-permute-start.5 = (bf16[64,1,128]{2,0,1:T(8,128)(2,1)S(1)}, bf16[64,1,128]{2,0,1:T(8,128)(2,1)S(1)}, u32[]{:S(2)}, u32[]{:S(2)}) collective-permute-start(bf16[64,1,128]{2,0,1:T(8,128)(2,1)S(1)} %get-tuple-element.36), channel_id=1, source_target_pairs={{16,0},{17,1},{18,2},{19,3},{20,4},{21,5},{22,6},{23,7},{24,8},{25... | collective-permute-start | bytes 49160 | tf_op jit(solution)/shard_map/ppermute | solution.py:29
  62.9 8.9 %collective-permute-start.6 = (bf16[64,26,1]{2,0,1:T(8,128)(2,1)S(1)}, bf16[64,26,1]{2,0,1:T(8,128)(2,1)S(1)}, u32[]{:S(2)}, u32[]{:S(2)}) collective-permute-start(bf16[64,26,1]{2,0,1:T(8,128)(2,1)S(1)} %get-tuple-element.25), channel_id=1, source_target_pairs={{0,4},{4,8},{8,12},{1,5},{5,9},{9,13},{2,6},{6,10},{10,14},{3,7},{... | collective-permute-start | bytes 9992 | tf_op jit(solution)/shard_map/ppermute | solution.py:26
  69.7 4.4 %collective-permute-start.7 = (bf16[64,26,1]{2,0,1:T(8,128)(2,1)S(1)}, bf16[64,26,1]{2,0,1:T(8,128)(2,1)S(1)}, u32[]{:S(2)}, u32[]{:S(2)}) collective-permute-start(bf16[64,26,1]{2,0,1:T(8,128)(2,1)S(1)} %get-tuple-element.26), channel_id=1, source_target_pairs={{4,0},{8,4},{12,8},{5,1},{9,5},{13,9},{6,2},{10,6},{14,10},{7,3},{... | collective-permute-start | bytes 9992 | tf_op jit(solution)/shard_map/ppermute | solution.py:29
  77.8 2.9 %copy-start.11 = (bf16[256,24,128]{0,2,1:T(8,128)(2,1)}, bf16[256,24,128]{0,2,1:T(8,128)(2,1)S(1)}, u32[]{:S(2)}) copy-start(bf16[256,24,128]{0,2,1:T(8,128)(2,1)S(1)} %get-tuple-element.64) | copy-start | bytes 4718596
  84.4 7.0 %copy-start.17 = (f32[9,64,64]{2,1,0:T(8,128)}, f32[9,64,64]{2,1,0:T(8,128)S(1)}, u32[]{:S(2)}) copy-start(f32[9,64,64]{2,1,0:T(8,128)S(1)} %fusion.54) | copy-start | bytes 442372
  84.4 11.0 %collective-permute-start.9 = (bf16[64,1,128]{2,0,1:T(8,128)(2,1)}, bf16[64,1,128]{2,0,1:T(8,128)(2,1)S(1)}, u32[]{:S(2)}, u32[]{:S(2)}) collective-permute-start(bf16[64,1,128]{2,0,1:T(8,128)(2,1)} %get-tuple-element.34), channel_id=1, source_target_pairs={{16,0},{17,1},{18,2},{19,3},{20,4},{21,5},{22,6},{23,7},{24,8},{25... | collective-permute-start | bytes 49160 | tf_op jit(solution)/shard_map/ppermute | solution.py:29
  85.7 9.7 %collective-permute-start.8 = (bf16[64,1,128]{2,0,1:T(8,128)(2,1)}, bf16[64,1,128]{2,0,1:T(8,128)(2,1)S(1)}, u32[]{:S(2)}, u32[]{:S(2)}) collective-permute-start(bf16[64,1,128]{2,0,1:T(8,128)(2,1)} %get-tuple-element.33), channel_id=1, source_target_pairs={{0,16},{1,17},{2,18},{3,19},{4,20},{5,21},{6,22},{7,23},{8,24},{9,... | collective-permute-start | bytes 49160 | tf_op jit(solution)/shard_map/ppermute | solution.py:26
  92.8 12.7 %copy-start.57 = (bf16[64,64,1]{1,0,2:T(8,128)(2,1)S(1)}, bf16[64,64,1]{1,0,2:T(8,128)(2,1)}, u32[]{:S(2)}) copy-start(bf16[64,64,1]{1,0,2:T(8,128)(2,1)} %reshape.252) | copy-start | bytes 24580
  95.4 10.3 %copy-start.58 = (bf16[64,64,1]{1,0,2:T(8,128)(2,1)S(1)}, bf16[64,64,1]{1,0,2:T(8,128)(2,1)}, u32[]{:S(2)}) copy-start(bf16[64,64,1]{1,0,2:T(8,128)(2,1)} %reshape.258) | copy-start | bytes 24580
  95.7 10.3 %collective-permute-start.10 = (bf16[64,26,1]{2,0,1:T(8,128)(2,1)S(1)}, bf16[64,26,1]{2,0,1:T(8,128)(2,1)S(1)}, u32[]{:S(2)}, u32[]{:S(2)}) collective-permute-start(bf16[64,26,1]{2,0,1:T(8,128)(2,1)S(1)} %get-tuple-element.21), channel_id=1, source_target_pairs={{4,0},{8,4},{12,8},{5,1},{9,5},{13,9},{6,2},{10,6},{14,10},{7,3},{... | collective-permute-start | bytes 9992 | tf_op jit(solution)/shard_map/ppermute | solution.py:29
  97.0 9.6 %collective-permute-start.11 = (bf16[64,26,1]{2,0,1:T(8,128)(2,1)S(1)}, bf16[64,26,1]{2,0,1:T(8,128)(2,1)S(1)}, u32[]{:S(2)}, u32[]{:S(2)}) collective-permute-start(bf16[64,26,1]{2,0,1:T(8,128)(2,1)S(1)} %get-tuple-element.22), channel_id=1, source_target_pairs={{0,4},{4,8},{8,12},{1,5},{5,9},{9,13},{2,6},{6,10},{10,14},{3,7},{... | collective-permute-start | bytes 9992 | tf_op jit(solution)/shard_map/ppermute | solution.py:26
  116.3 6.7 %copy-start.50 = (bf16[64,64,1]{1,0,2:T(8,128)(2,1)S(1)}, bf16[64,64,1]{1,0,2:T(8,128)(2,1)}, u32[]{:S(2)}) copy-start(bf16[64,64,1]{1,0,2:T(8,128)(2,1)} %reshape.265) | copy-start | bytes 24580
  117.2 7.0 %copy-start.16 = (f32[9,64,64]{2,1,0:T(8,128)}, f32[9,64,64]{2,1,0:T(8,128)S(1)}, u32[]{:S(2)}) copy-start(f32[9,64,64]{2,1,0:T(8,128)S(1)} %fusion.61) | copy-start | bytes 442372
  117.2 9.8 %collective-permute-start.13 = (bf16[64,1,128]{2,0,1:T(8,128)(2,1)}, bf16[64,1,128]{2,0,1:T(8,128)(2,1)S(1)}, u32[]{:S(2)}, u32[]{:S(2)}) collective-permute-start(bf16[64,1,128]{2,0,1:T(8,128)(2,1)} %get-tuple-element.32), channel_id=1, source_target_pairs={{16,0},{17,1},{18,2},{19,3},{20,4},{21,5},{22,6},{23,7},{24,8},{25... | collective-permute-start | bytes 49160 | tf_op jit(solution)/shard_map/ppermute | solution.py:29
  118.5 8.5 %collective-permute-start.12 = (bf16[64,1,128]{2,0,1:T(8,128)(2,1)}, bf16[64,1,128]{2,0,1:T(8,128)(2,1)S(1)}, u32[]{:S(2)}, u32[]{:S(2)}) collective-permute-start(bf16[64,1,128]{2,0,1:T(8,128)(2,1)} %get-tuple-element.31), channel_id=1, source_target_pairs={{0,16},{1,17},{2,18},{3,19},{4,20},{5,21},{6,22},{7,23},{8,24},{9,... | collective-permute-start | bytes 49160 | tf_op jit(solution)/shard_map/ppermute | solution.py:26
  124.6 11.5 %copy-start.48 = (bf16[64,64,1]{1,0,2:T(8,128)(2,1)S(1)}, bf16[64,64,1]{1,0,2:T(8,128)(2,1)}, u32[]{:S(2)}) copy-start(bf16[64,64,1]{1,0,2:T(8,128)(2,1)} %reshape.262) | copy-start | bytes 24580
  127.1 9.2 %copy-start.49 = (bf16[64,64,1]{1,0,2:T(8,128)(2,1)S(1)}, bf16[64,64,1]{1,0,2:T(8,128)(2,1)}, u32[]{:S(2)}) copy-start(bf16[64,64,1]{1,0,2:T(8,128)(2,1)} %reshape.268) | copy-start | bytes 24580
  127.3 10.1 %collective-permute-start.14 = (bf16[64,26,1]{2,0,1:T(8,128)(2,1)S(1)}, bf16[64,26,1]{2,0,1:T(8,128)(2,1)S(1)}, u32[]{:S(2)}, u32[]{:S(2)}) collective-permute-start(bf16[64,26,1]{2,0,1:T(8,128)(2,1)S(1)} %get-tuple-element.17), channel_id=1, source_target_pairs={{4,0},{8,4},{12,8},{5,1},{9,5},{13,9},{6,2},{10,6},{14,10},{7,3},{... | collective-permute-start | bytes 9992 | tf_op jit(solution)/shard_map/ppermute | solution.py:29
  128.6 8.8 %collective-permute-start.15 = (bf16[64,26,1]{2,0,1:T(8,128)(2,1)S(1)}, bf16[64,26,1]{2,0,1:T(8,128)(2,1)S(1)}, u32[]{:S(2)}, u32[]{:S(2)}) collective-permute-start(bf16[64,26,1]{2,0,1:T(8,128)(2,1)S(1)} %get-tuple-element.18), channel_id=1, source_target_pairs={{0,4},{4,8},{8,12},{1,5},{5,9},{9,13},{2,6},{6,10},{10,14},{3,7},{... | collective-permute-start | bytes 9992 | tf_op jit(solution)/shard_map/ppermute | solution.py:26
  (32 other events, 51.4 us)

commit v2 on v1

--- a/solution.py
+++ b/solution.py
@@ -16,19 +16,6 @@
 beta_two = 0.99
 learn_rate = 0.0001
 weight_decay = 0.1
-
-
-def extended(block, sides, width):
-    for axis, dim in sides:
-        count = lax.axis_size(axis)
-        forward = [(i, i + 1) for i in range(count - 1)]
-        backward = [(target, source) for source, target in forward]
-        low = lax.ppermute(
-            lax.slice_in_dim(block, block.shape[dim] - width, None, axis=dim), axis, forward
-        )
-        high = lax.ppermute(lax.slice_in_dim(block, 0, width, axis=dim), axis, backward)
-        block = jnp.concatenate([low, block, high], axis=dim)
-    return block
 
 
 def unpack(weights):
@@ -46,28 +33,6 @@
         )
     head = weights[offset:].reshape(C, CLASSES)
     return (blocks_list, head)
-
-
-def forward_rim(field):
-    return extended(field, (("row", 1), ("col", 2)), 1)
-
-
-def backward_rim(field):
-    return extended(field, (("row", 1), ("col", 2)), 1)
-
-
-def conv_taps(w_mid, padded, height, width):
-    total = jnp.zeros((w_mid.shape[2], height, width), jnp.float32)
-    for position in range(9):
-        shift_row = position // 3
-        shift_col = position % 3
-        total = total + jnp.einsum(
-            "io,ihw->ohw",
-            w_mid[position],
-            padded[:, shift_row : shift_row + height, shift_col : shift_col + width],
-            preferred_element_type=jnp.float32,
-        )
-    return total
 
 
 MESH_ID = pl.DeviceIdType.MESH
@@ -237,99 +202,263 @@
     return out[0], out[1], out[2], total[1, 0]
 
 
+def directions():
+    return [(-1, 0), (1, 0), (0, -1), (0, 1), (-1, -1), (1, -1), (-1, 1), (1, 1)]
+
+
+def opposite(number):
+    dr, dc = directions()[number]
+    return directions().index((-dr, -dc))
+
+
+SENT = (0, 1, 2, 3, 2, 2, 3, 3)
+
+
+def near(sizes, number):
+    nrow, ncol, _ = sizes
+    dr, dc = directions()[number]
+    row, col, dp = (lax.axis_index(a) for a in AXES)
+    r, c = row + dr, col + dc
+    there = jnp.logical_and(jnp.logical_and(r >= 0, r < nrow), jnp.logical_and(c >= 0, c < ncol))
+    return there, (r, c, dp)
+
+
+def dot(a, b):
+    return lax.dot_general(a, b, (((1,), (0,)), ((), ())), preferred_element_type=jnp.float32)
+
+
+def dot_t(a, b):
+    return lax.dot_general(a, b, (((1,), (1,)), ((), ())), preferred_element_type=jnp.float32)
+
+
+def bottleneck_kernel(
+    sizes, height, tiles, x_ref, hot_ref, head_ref,
+    wit1, af1, wot1, ab1, wo1, wit2, af2, wot2, ab2, wo2, wi2,
+    gin1, gmid1, gout1, gin2, gmid2, gout2, ghead, loss_ref,
+    s1, s2, d1, d2, z1, z2, h21, h22, y1, y2, sent, got, send_sem, recv_sem,
+):
+    f32, bf16 = jnp.float32, jnp.bfloat16
+    lane = lax.broadcasted_iota(jnp.int32, (MID, 128), 1)
+    step = 8 if height % 8 == 0 else height
+    size = step * 128
+    chunks = [slice(j * size, (j + 1) * size) for j in range(height // step)]
+    own = slice(MID, 2 * MID)
+
+    def inner(part):
+        return slice(part.start + 128, part.stop + 128)
+
+    got[...] = jnp.zeros_like(got)
+    for z in (z1, z2):
+        z[:, 0:256] = jnp.zeros((MID, 256), bf16)
+        z[:, (height + 2) * 128 :] = jnp.zeros((MID, 256), bf16)
+    barrier = pltpu.get_barrier_semaphore()
+    for number in range(8):
+        there, where = near(sizes, number)
+
+        @pl.when(there)
+        def _():
+            pl.semaphore_signal(barrier, inc=1, device_id=where, device_id_type=MESH_ID)
+
+    around = sum(near(sizes, number)[0].astype(jnp.int32) for number in range(8))
+    pl.semaphore_wait(barrier, around)
+
+    def copy(turn, number, slot):
+        _, where = near(sizes, number)
+        return pltpu.make_async_remote_copy(
+            src_ref=sent.at[turn, SENT[number]], dst_ref=got.at[turn, slot],
+            send_sem=send_sem.at[turn, number], recv_sem=recv_sem.at[turn, slot],
+            device_id=where, device_id_type=MESH_ID)
+
+    def rim_start(field, turn):
+        sent[turn, 0] = field[own, 128:256]
+        sent[turn, 1] = field[own, height * 128 : (height + 1) * 128]
+        left = jnp.zeros((MID, 128), f32)
+        right = jnp.zeros((MID, 128), f32)
+        for y in range(1, height + 1):
+            line = field[own, y * 128 : (y + 1) * 128].astype(f32)
+            left = jnp.where(lane == y, pltpu.roll(line, y, 1), left)
+            right = jnp.where(lane == y, pltpu.roll(line, (y + 1) % 128, 1), right)
+        sent[turn, 2] = left.astype(bf16)
+        sent[turn, 3] = right.astype(bf16)
+        for number in range(8):
+            there, _ = near(sizes, number)
+
+            @pl.when(there)
+            def _():
+                copy(turn, number, opposite(number)).start()
+
+    def rim_finish(field, turn):
+        for number in range(8):
+            there, _ = near(sizes, number)
+
+            @pl.when(there)
+            def _():
+                copy(turn, number, opposite(number)).wait_send()
+                copy(turn, number, number).wait_recv()
+
+        field[own, 0:128] = got[turn, 0]
+        field[own, (height + 1) * 128 :] = got[turn, 1]
+
+        def column(side, low, high):
+            low = pltpu.roll(got[turn, low].astype(f32), 128 - height, 1)
+            high = pltpu.roll(got[turn, high].astype(f32), height, 1)
+            middle = jnp.where(lane == height + 1, high, got[turn, side].astype(f32))
+            return jnp.where(lane == 0, low, middle)
+
+        left = column(2, 4, 5)
+        right = column(3, 6, 7)
+        for y in range(height + 2):
+            part = slice(y * 128, (y + 1) * 128)
+            line = field[own, part].astype(f32)
+            before = jnp.where(lane == 0, left[:, y : y + 1], pltpu.roll(line, 1, 1))
+            after = jnp.where(lane == 127, right[:, y : y + 1], pltpu.roll(line, 127, 1))
+            field[0:MID, part] = before.astype(bf16)
+            field[2 * MID :, part] = after.astype(bf16)
+
+    def conv(w, field, part, reverse):
+        wide = dot(w[...], field[:, part.start : part.stop + 256])
+        total = None
+        for r in range(3):
+            at = (2 - r if reverse else r) * 128
+            term = wide[r * MID : (r + 1) * MID, at : at + size]
+            total = term if total is None else total + term
+        return total
+
+    def relu(value):
+        return jnp.maximum(value, 0.0)
+
+    for part in chunks:
+        s1[own, inner(part)] = relu(dot(wit1[...], x_ref[:, part])).astype(bf16)
+    rim_start(s1, 0)
+    rim_finish(s1, 0)
+    for part in chunks:
+        h2 = relu(conv(af1, s1, part, False)).astype(bf16)
+        h21[:, part] = h2
+        y = relu(dot(wot1[...], h2) + x_ref[:, part].astype(f32)).astype(bf16)
+        y1[:, part] = y
+        s2[own, inner(part)] = relu(dot(wit2[...], y)).astype(bf16)
+    rim_start(s2, 1)
+    rim_finish(s2, 1)
+    pool = jnp.zeros((C, 128), f32)
+    for part in chunks:
+        h2 = relu(conv(af2, s2, part, False)).astype(bf16)
+        h22[:, part] = h2
+        y = relu(dot(wot2[...], h2) + y1[:, part].astype(f32)).astype(bf16)
+        y2[:, part] = y
+        y = y.astype(f32)
+        for k in range(step):
+            pool = pool + y[:, k * 128 : (k + 1) * 128]
+
+    wide_lane = lax.broadcasted_iota(jnp.int32, (C, 128), 1)
+    one_lane = lax.broadcasted_iota(jnp.int32, (1, 128), 1)
+    valid = one_lane < CLASSES
+    head = head_ref[...]
+    head_grad = jnp.zeros((C, 128), f32)
+    upstream = jnp.zeros((C, 128), f32)
+    loss = jnp.zeros((1, 1), f32)
+    for t in range(128 // TILE_COLS):
+        mine = wide_lane // TILE_COLS == t
+        pooled = jnp.sum(jnp.where(mine, pool, 0.0), axis=1, keepdims=True) / (TILE_ROWS * TILE_COLS)
+        logits = jnp.sum(pooled * head, axis=0, keepdims=True)
+        highest = jnp.max(jnp.where(valid, logits, -jnp.inf), axis=1, keepdims=True)
+        power = jnp.where(valid, jnp.exp(jnp.where(valid, logits - highest, 0.0)), 0.0)
+        spread = jnp.sum(power, axis=1, keepdims=True)
+        onehot = hot_ref[t : t + 1, :]
+        loss = loss + jnp.log(spread) + highest - jnp.sum(onehot * logits, axis=1, keepdims=True)
+        dlogits = (power / spread - onehot) / tiles
+        head_grad = head_grad + pooled * dlogits
+        dpool = jnp.sum(dlogits * head, axis=1, keepdims=True) / (TILE_ROWS * TILE_COLS)
+        upstream = jnp.where(mine, dpool, upstream)
+    ghead[...] = head_grad
+    loss_ref[...] = jnp.broadcast_to(loss, (8, 128))
+    upstream = upstream.astype(bf16).astype(f32)
+
+    for part in chunks:
+        for k in range(step):
+            line = slice(part.start + k * 128, part.start + (k + 1) * 128)
+            y2[:, line] = jnp.where(y2[:, line].astype(f32) > 0, upstream, 0.0).astype(bf16)
+        dg2 = dot(wo2[...], y2[:, part])
+        dg2 = jnp.where(h22[:, part].astype(f32) > 0, dg2, 0.0).astype(bf16)
+        d2[own, inner(part)] = dg2
+        z2[:, part.start + 256 : part.stop + 256] = dg2
+    rim_start(d2, 2)
+    gout2[...] = dot_t(h22[...], y2[...])
+
+    def mid_grad(field, z):
+        grid = [z[:, (2 - r) * 128 : (2 - r + height + 2) * 128] for r in range(3)]
+        return dot_t(field[...], jnp.concatenate(grid, axis=0))
+
+    gmid2[...] = mid_grad(s2, z2)
+    rim_finish(d2, 2)
+    grad = jnp.zeros((C, MID), f32)
+    for part in chunks:
+        dg1 = conv(ab2, d2, part, True)
+        dg1 = jnp.where(s2[own, inner(part)].astype(f32) > 0, dg1, 0.0).astype(bf16)
+        grad = grad + dot_t(y1[:, part], dg1)
+        dy = (dot(wi2[...], dg1) + y2[:, part].astype(f32)).astype(bf16).astype(f32)
+        dz = jnp.where(y1[:, part].astype(f32) > 0, dy, 0.0).astype(bf16)
+        y2[:, part] = dz
+        dg2 = dot(wo1[...], dz)
+        dg2 = jnp.where(h21[:, part].astype(f32) > 0, dg2, 0.0).astype(bf16)
+        d1[own, inner(part)] = dg2
+        z1[:, part.start + 256 : part.stop + 256] = dg2
+    gin2[...] = grad
+    rim_start(d1, 3)
+    gout1[...] = dot_t(h21[...], y2[...])
+    gmid1[...] = mid_grad(s1, z1)
+    rim_finish(d1, 3)
+    grad = jnp.zeros((C, MID), f32)
+    for part in chunks:
+        dg1 = conv(ab1, d1, part, True)
+        dg1 = jnp.where(s1[own, inner(part)].astype(f32) > 0, dg1, 0.0).astype(bf16)
+        grad = grad + dot_t(x_ref[:, part], dg1)
+    gin1[...] = grad
+
+
 def local(image, labels, weights, momentum):
-    inputs = image[0]
-    label_grid = labels[0]
-    height, width = (inputs.shape[1], inputs.shape[2])
+    sizes = tuple(lax.axis_size(a) for a in AXES)
+    height, width = image.shape[2], image.shape[3]
+    assert width == 128 and height == TILE_ROWS and height + 2 < 128
+    f32, bf16 = jnp.float32, jnp.bfloat16
     blocks_list, head = unpack(weights)
-    total_tiles = (
-        label_grid.shape[0]
-        * label_grid.shape[1]
-        * lax.axis_size("row")
-        * lax.axis_size("col")
-        * lax.axis_size("dp")
-    )
-    stored = []
+    total_tiles = labels.shape[1] * labels.shape[2] * sizes[0] * sizes[1] * sizes[2]
+    x = image[0].reshape(C, height * width)
+    hot = labels[0, 0][:, None] == jnp.arange(128, dtype=jnp.int32)
+    hot = jnp.pad(hot.astype(f32), ((0, 8 - hot.shape[0]), (0, 0)))
+    head = jnp.pad(head, ((0, 0), (0, 128 - CLASSES)))
+    packed = []
     for w_in, w_mid, w_out in blocks_list:
-        h_first = jnp.maximum(
-            jnp.einsum("io,ihw->ohw", w_in, inputs, preferred_element_type=jnp.float32), 0.0
-        ).astype(jnp.bfloat16)
-        padded = forward_rim(h_first)
-        h_second = jnp.maximum(conv_taps(w_mid, padded, height, width), 0.0).astype(jnp.bfloat16)
-        output = jnp.maximum(
-            jnp.einsum("io,ihw->ohw", w_out, h_second, preferred_element_type=jnp.float32)
-            + inputs.astype(jnp.float32),
-            0.0,
-        ).astype(jnp.bfloat16)
-        kept = padded
-        stored.append((inputs, kept, h_second, output))
-        inputs = output
-    tiles_a = height // TILE_ROWS
-    tiles_b = width // TILE_COLS
-    pooled = jnp.mean(
-        inputs.astype(jnp.float32).reshape(C, tiles_a, TILE_ROWS, tiles_b, TILE_COLS), axis=(2, 4)
-    )
-    logits = jnp.einsum("cab,ck->abk", pooled, head, precision=lax.Precision.HIGHEST)
-    highest = jnp.max(logits, axis=-1, keepdims=True)
-    logsum = jnp.log(jnp.sum(jnp.exp(logits - highest), axis=-1, keepdims=True)) + highest
-    onehot = (label_grid[:, :, None] == jnp.arange(CLASSES, dtype=jnp.int32)).astype(jnp.float32)
-    loss_part = jnp.sum(logsum[:, :, 0] - jnp.sum(onehot * logits, axis=-1))
-    dlogits = (jnp.exp(logits - logsum) - onehot) / total_tiles
-    grad_head = jnp.einsum("cab,abk->ck", pooled, dlogits, precision=lax.Precision.HIGHEST)
-    dpooled = jnp.einsum("abk,ck->cab", dlogits, head, precision=lax.Precision.HIGHEST) / (
-        TILE_ROWS * TILE_COLS
-    )
-    upstream = (
-        jnp.broadcast_to(dpooled[:, :, None, :, None], (C, tiles_a, TILE_ROWS, tiles_b, TILE_COLS))
-        .reshape(C, height, width)
-        .astype(jnp.bfloat16)
-    )
-    grads = [None, None]
-    for number in (1, 0):
-        w_in, w_mid, w_out = blocks_list[number]
-        inputs, kept, h_second, output = stored[number]
-        padded = kept
-        d_sum = jnp.where(output > 0, upstream, jnp.zeros_like(upstream))
-        grad_out = jnp.einsum("ihw,ohw->io", h_second, d_sum, preferred_element_type=jnp.float32)
-        d_second = jnp.einsum("io,ohw->ihw", w_out, d_sum, preferred_element_type=jnp.float32)
-        d_second = jnp.where(h_second > 0, d_second, 0.0).astype(jnp.bfloat16)
-        spread_back = backward_rim(d_second)
-        grad_mid = jnp.stack(
-            [
-                jnp.einsum(
-                    "ihw,ohw->io",
-                    padded[
-                        :,
-                        position // 3 : position // 3 + height,
-                        position % 3 : position % 3 + width,
-                    ],
-                    d_second,
-                    preferred_element_type=jnp.float32,
-                )
-                for position in range(9)
-            ]
-        )
-        d_first = jnp.zeros((MID, height, width), jnp.float32)
-        for position in range(9):
-            shift_row = 2 - position // 3
-            shift_col = 2 - position % 3
-            d_first = d_first + jnp.einsum(
-                "io,ohw->ihw",
-                w_mid[position],
-                spread_back[:, shift_row : shift_row + height, shift_col : shift_col + width],
-                preferred_element_type=jnp.float32,
-            )
-        h_first = padded[:, 1:-1, 1:-1]
-        d_first = jnp.where(h_first > 0, d_first, 0.0).astype(jnp.bfloat16)
-        grad_in = jnp.einsum("ihw,ohw->io", inputs, d_first, preferred_element_type=jnp.float32)
-        if number == 1:
-            upstream = (
-                jnp.einsum("io,ohw->ihw", w_in, d_first, preferred_element_type=jnp.float32)
-                + d_sum.astype(jnp.float32)
-            ).astype(jnp.bfloat16)
-        grads[number] = jnp.concatenate([grad_in.ravel(), grad_mid.ravel(), grad_out.ravel()])
-    flat = jnp.concatenate([grads[0], grads[1], grad_head.ravel()])
-    new_weights, new_momentum, update, loss_total = lion_step(flat, loss_part, weights, momentum)
+        taps = w_mid.reshape(3, 3, MID, MID)
+        forth = taps.transpose(0, 3, 1, 2).reshape(3 * MID, 3 * MID)
+        back = taps[:, ::-1].transpose(0, 2, 1, 3).reshape(3 * MID, 3 * MID)
+        packed += [w_in.T, forth, w_out.T, back, w_out]
+    packed.append(blocks_list[1][0])
+    grads = [(C, MID), (3 * MID, 3 * MID), (MID, C)] * 2 + [(C, 128), (8, 128)]
+    vmem = pl.BlockSpec(memory_space=pltpu.VMEM)
+    wide = height * 128
+    field = pltpu.VMEM((3 * MID, wide + 256), bf16)
+    spaced = pltpu.VMEM((MID, wide + 512), bf16)
+    slim = pltpu.VMEM((MID, wide), bf16)
+    full = pltpu.VMEM((C, wide), bf16)
+    gin1, gmid1, gout1, gin2, gmid2, gout2, ghead, loss = pl.pallas_call(
+        lambda *refs: bottleneck_kernel(sizes, height, total_tiles, *refs),
+        out_shape=[jax.ShapeDtypeStruct(g, f32) for g in grads],
+        in_specs=[vmem] * (3 + len(packed)),
+        out_specs=[vmem] * len(grads),
+        scratch_shapes=[
+            field, field, field, field, spaced, spaced, slim, slim, full, full,
+            pltpu.VMEM((4, 4, MID, 128), bf16), pltpu.VMEM((4, 8, MID, 128), bf16),
+            pltpu.SemaphoreType.DMA((4, 8)), pltpu.SemaphoreType.DMA((4, 8)),
+        ],
+        compiler_params=pltpu.CompilerParams(
+            collective_id=1, has_side_effects=True, vmem_limit_bytes=48 * 1024 * 1024),
+    )(x, hot, head, *packed)
+    flat = []
+    for gin, gmid, gout in ((gin1, gmid1, gout1), (gin2, gmid2, gout2)):
+        gmid = gmid.reshape(3 * MID, 3, MID).transpose(1, 0, 2)
+        flat += [gin.ravel(), gmid.ravel(), gout.ravel()]
+    flat = jnp.concatenate(flat + [ghead[:, :CLASSES].ravel()])
+    new_weights, new_momentum, update, loss_total = lion_step(flat, loss[0, 0], weights, momentum)
     return (new_weights, new_momentum, update, loss_total / total_tiles)
 
 

time: 183 us -> 62.6 us (0.34)
  starting transfers between devices: 53.8 us -> 0 us
  matrix products: 36.2 us -> 0 us
  local copies, waits for them, and re-layouts: 37.1 us -> 7.34 us
  Pallas kernels: 32.3 us -> 50.5 us
  waiting for transfers between devices: 9.47 us -> 0 us
  other arithmetic: 8.32 us -> 1.82 us
    ppermute x16 -> x0, starting transfers between devices: 53.8 us -> none  [the longest x8 43.3 us: extended(): lax.ppermute(lax.slice_in_dim(block, block.shape[dim] - width, None, axis...]
    dot_general x67 -> x0, matrix products: 36.2 us -> none  [the longest x17 10.4 us: local(): jnp.einsum('io,ohw->ihw', w_mid[position], spread_back[:, shift_row:shift...]
    pallas_call x0 -> x1, Pallas kernels: none -> 25.6 us  [local(): pl.pallas_call(lambda *refs: bottleneck_kernel(sizes, height, total_tiles...]
    squeeze x37 -> x0, local copies, waits for them, and re-layouts: 16.6 us -> none  [the longest x32 12.9 us: conv_taps(): w_mid[position]]
    ppermute x16 -> x0, waiting for transfers between devices: 9.47 us -> none  [the longest x8 8.85 us: extended(): lax.ppermute(lax.slice_in_dim(block, 0, width, axis=dim), axis, backward)]
    pallas_call x1, Pallas kernels: 32.3 us -> 24.9 us  [lion_step(): pl.pallas_call(lambda *refs: lion_kernel(sizes, share, params, *refs), ou...]
    unnamed x138 -> x16, local copies, waits for them, and re-layouts: 8.67 us -> 1.89 us
    concatenate x8 -> x0, other arithmetic: 4.13 us -> none  [extended(): block = jnp.concatenate([low, block, high], axis=dim)]
  transfers between devices with their start and end apart: 16 -> 0, of which waited for: 4 -> 0; matrix products, arithmetic and copies ran while one was open for 20% -> 0% of each run, Pallas kernels for 0% -> 0%
where the time goes in v2:
time: 62.6 us; the launch traced here: 62.4 us
  Pallas kernels  50.5 us (81%)
  local copies, waits for them, and re-layouts  7.34 us (12%)
  between operations  2.8 us (4%)
  other arithmetic  1.82 us (3%)
    pallas_call x1, Pallas kernels, local(): pl.pallas_call(lambda *refs: bottleneck_kernel(sizes, height, total_tiles...  25.6 us
    pallas_call x1, Pallas kernels, lion_step(): pl.pallas_call(lambda *refs: lion_kernel(sizes, share, params, *refs), ou...  24.9 us
    unnamed x16, local copies, waits for them, and re-layouts  1.89 us
    slice x2, local copies, waits for them, and re-layouts, lion_step(): return (out[0], out[1], out[2], total[1, 0])  1.32 us

profile of v2, /device:TPU:0, one launch (start us, length us, event | category | flops | bytes accessed | tf_op | source)
XLA Modules:
  0.0 62.4 jit_solution(13854330791583596873)
XLA Ops:
  0.6 1.1 %convert.10 = bf16[141312]{0:T(1024)(128)(2,1)S(1)} convert(f32[141312]{0:T(1024)} %param.6) | non-fusion elementwise | flops 141312 | bytes 847872 | tf_op jit(solution)/shard_map/convert.7
  1.7 0.1 convert_element_type.31.refs_13_
  1.8 0.1 copy.16
  2.0 0.1 copy.19.refs_5_
  2.1 0.1 copy.20.refs_10_
  2.2 0.1 convert_element_type.28
  2.3 0.1 copy.13
  2.4 0.1 convert_element_type.29
  2.6 0.1 copy.15
  2.7 0.2 reshape.132.refs_6_
  2.9 0.1 convert_element_type.32
  3.0 0.1 copy.18
  3.1 0.2 reshape.134.refs_11_
  3.3 0.2 copy.14
  3.5 0.2 reshape.131.refs_4_
  3.6 0.2 copy.17
  3.8 0.2 reshape.133.refs_9_
  4.0 0.0 slice-start
  4.0 0.0 copy-start.2
  4.0 1.7 %copy.31 = bf16[32,8,24,128]{3,1,2,0:T(8,128)(2,1)S(1)} copy(bf16[32,8,24,128]{3,2,1,0:T(8,128)(2,1)} %bitcast.47) | data formatting | bytes 3145728
  5.7 0.0 slice-done
  5.7 0.1 slice.88
  5.9 0.0 copy-done.2
  5.9 0.1 iota_compare_fusion
  6.0 25.6 %shard_map.75 = (f32[256,64]{1,0:T(8,128)S(1)}, f32[192,192]{1,0:T(8,128)S(1)}, f32[64,256]{1,0:T(8,128)S(1)}, f32[256,64]{1,0:T(8,128)S(1)}, f32[192,192]{1,0:T...) custom-call(bf16[256,3072]{1,0:T(8,128)(2,1)S(1)} %bitcast.36, ...), custom_call_target="tpu_custom_call" | custom-call | tf_op jit(solution)/shard_map/pallas_call | solution.py:443
  31.5 0.1 copy.21
  31.7 0.1 copy.22
  31.8 0.1 reshape.137
  31.9 0.1 reshape.135
  32.0 0.0 copy-start.1
  32.0 0.0 copy-start
  32.1 0.1 reshape.139
  32.2 0.1 copy.23
  32.4 0.1 copy.24
  32.5 0.1 reshape.141
  32.7 0.1 reshape.143
  32.8 0.0 copy-done.1
  32.9 0.4 dynamic_update_slice.3
  33.2 0.0 copy-done
  33.2 0.5 slice.96
  33.7 0.6 %compare_select_fusion.refs_1_ = f32[1,128]{1,0:T(1,128)S(1)} fusion(f32[]{:T(128)} %bitcast.14), kind=kLoop, calls=%fused_computation.15 | loop fusion | flops 256 | bytes 516 | tf_op jit(solution)/shard_map/jit(_where)/select_n | solution.py:171
  34.4 24.9 %shard_map.76 = (f32[3,35,128]{2,1,0:T(8,128)S(1)}, f32[8,128]{1,0:T(8,128)S(1)}) custom-call(f32[1104,128]{1,0:T(8,128)S(1)} %bitcast.37, f32[1,128]{1,0:T(1,128)S(1)} %compare_select_fusion.refs_1_, f32[35,128]{1,0:T(8,128)S(1)} %bitcast.43, f32[35,128]{1,0:T(8,128)S(1)} %constant_dynamic-slice_fusion.refs_3_), custom_call_target="tpu_custom_call" | custom-call | tf_op jit(solution)/shard_map/pallas_call | solution.py:184
  59.3 0.8 %dynamic-slice_reduce_fusion = (f32[4416]{0:T(1024)}, f32[4416]{0:T(1024)}, f32[4416]{0:T(1024)}) fusion(f32[3,4480]{1,0:T(4,128)S(1)} %bitcast.55, s32[]{:T(128)S(6)} %add.29, s32[]{:T(128)S(6)} %select_n.24, s32[]{:T(128)S(6)} %add.28), kind=kLoop, calls=%fused_computation.4 | loop fusion | bytes 105996 | tf_op jit(solution)/shard_map/slice | solution.py:202
  60.1 0.5 slice.100
  (20 shorter events, 0.3 us)
Async XLA Ops:
  4.0 1.8 %slice-start = ((f32[141312]{0:T(1024)}), f32[2048]{0:T(1024)S(1)}, s32[]{:S(2)}) async-start(f32[141312]{0:T(1024)} %param.6), calls=%async_computation | async-start | bytes 16384 | tf_op jit(solution)/shard_map/slice | solution.py:34
  4.0 1.9 %copy-start.2 = (s32[1,1,2]{2,1,0:T(1,128)S(1)}, s32[1,1,2]{2,1,0:T(1,128)}, u32[]{:S(2)}) copy-start(s32[1,1,2]{2,1,0:T(1,128)} %param.5) | copy-start | bytes 28
  32.0 0.8 %copy-start.1 = (f32[4416]{0:T(1024)S(1)}, f32[4416]{0:T(1024)}, u32[]{:S(2)}) copy-start(f32[4416]{0:T(1024)} %param.7) | copy-start | bytes 52996
  32.0 1.2 %copy-start = (f32[141312]{0:T(1024)S(1)}, f32[141312]{0:T(1024)}, u32[]{:S(2)}) copy-start(f32[141312]{0:T(1024)} %param.6) | copy-start | bytes 1695748

commit v3 on v2

--- a/solution.py
+++ b/solution.py
@@ -72,7 +72,6 @@
             pl.semaphore_signal(barrier, inc=1, device_id=target(k), device_id_type=MESH_ID)
             return carry
         lax.fori_loop(1, count, one, 0)
-    pl.semaphore_wait(barrier, nrow * ncol - 1 + ndp - 1)
 
 
 def exchange(count, source, landing, target, send, recv):
@@ -94,7 +93,7 @@
 
 
 def lion_kernel(sizes, share, params, flat_ref, loss_ref, mom_ref, wgt_ref, out_ref, total_ref,
-                held, a1, r1, a2, r2, a3, r3, r4, mine, rp, line_sum, rl, *sems):
+                held, a1, r1, a2, r2, r3, mine, rp, line_sum, rl, *sems):
     nrow, ncol, ndp = sizes
     lo_n = split_col(ncol)
     hi_n = ncol // lo_n
@@ -107,7 +106,8 @@
             for z in range(ndp):
                 start = ((r * ncol + c) * ndp + z) * share // 128
                 have = min(rows, flat_ref.shape[0] - start)
-                held[c % lo_n, r, c // lo_n, z, 0:have] = flat_ref[start : start + have, :]
+                held[c % lo_n, r * hi_n + c // lo_n, z, 0:have] = flat_ref[start : start + have, :]
+    pl.semaphore_wait(pltpu.get_barrier_semaphore(), nrow * ncol - 1 + ndp - 1)
 
     def step(count, me, now, landing, later, where, send, recv):
         exchange(count, lambda k: now.at[lax.rem(me + k, count)], landing,
@@ -120,9 +120,9 @@
         later[...] = total
 
     step(lo_n, lo, held, r1, a1, lambda p: (row, hi * lo_n + p, dp), sems[0], sems[1])
-    step(nrow, row, a1, r2, a2, lambda p: (p, col, dp), sems[2], sems[3])
-    step(hi_n, hi, a2, r3, a3, lambda p: (row, p * lo_n + lo, dp), sems[4], sems[5])
-    grad = step(ndp, dp, a3, r4, None, lambda p: (row, col, p), sems[6], sems[7])
+    step(nrow * hi_n, row * hi_n + hi, a1, r2, a2,
+         lambda p: (p // hi_n, lax.rem(p, hi_n) * lo_n + lo, dp), sems[2], sems[3])
+    grad = step(ndp, dp, a2, r3, None, lambda p: (row, col, p), sems[4], sems[5])
 
     me = (row * ncol + col) * ndp + dp
     skip = lax.rem(me * share, 128)
@@ -137,12 +137,12 @@
     which = lax.broadcasted_iota(jnp.int32, (8, 128), 0)
     mine[...] = jnp.where(which == 0, part, jnp.where(which == 1, loss_ref[...], 0.0))
     plane, line = peers(sizes)
-    exchange(nrow * ncol, lambda k: mine, rp, plane, sems[8], sems[9])
+    exchange(nrow * ncol, lambda k: mine, rp, plane, sems[6], sems[7])
     total = mine[...]
     for k in range(nrow * ncol - 1):
         total = total + rp[k]
     line_sum[...] = total
-    exchange(ndp, lambda k: line_sum, rl, line, sems[10], sems[11])
+    exchange(ndp, lambda k: line_sum, rl, line, sems[8], sems[9])
     for k in range(ndp - 1):
         total = total + rl[k]
     total_ref[...] = jnp.broadcast_to(jnp.sum(total, axis=1, keepdims=True), (8, 128))
@@ -174,7 +174,7 @@
     f32 = jnp.float32
     tail = (rows, 128)
     plane_n = nrow * ncol
-    counts = (lo_n, nrow, hi_n, ndp, plane_n, ndp)
+    counts = (lo_n, nrow * hi_n, ndp, plane_n, ndp)
     sems = [pltpu.SemaphoreType.DMA((max(n - 1, 1),)) for n in counts for _ in range(2)]
     vmem = pl.BlockSpec(memory_space=pltpu.VMEM)
 
@@ -187,10 +187,9 @@
         in_specs=[vmem] * 4,
         out_specs=(vmem, vmem),
         scratch_shapes=[
-            pltpu.VMEM((lo_n, nrow, hi_n, ndp) + tail, f32),
-            pltpu.VMEM((nrow, hi_n, ndp) + tail, f32), land(lo_n, nrow, hi_n, ndp),
-            pltpu.VMEM((hi_n, ndp) + tail, f32), land(nrow, hi_n, ndp),
-            pltpu.VMEM((ndp,) + tail, f32), land(hi_n, ndp),
+            pltpu.VMEM((lo_n, nrow * hi_n, ndp) + tail, f32),
+            pltpu.VMEM((nrow * hi_n, ndp) + tail, f32), land(lo_n, nrow * hi_n, ndp),
+            pltpu.VMEM((ndp,) + tail, f32), land(nrow * hi_n, ndp),
             land(ndp),
             pltpu.VMEM((8, 128), f32), pltpu.VMEM((max(plane_n - 1, 1), 8, 128), f32),
             pltpu.VMEM((8, 128), f32), pltpu.VMEM((max(ndp - 1, 1), 8, 128), f32),
@@ -287,6 +286,12 @@
             def _():
                 copy(turn, number, opposite(number)).start()
 
+        for y in range(1, height + 1):
+            part = slice(y * 128, (y + 1) * 128)
+            line = field[own, part].astype(f32)
+            field[0:MID, part] = pltpu.roll(line, 1, 1).astype(bf16)
+            field[2 * MID :, part] = pltpu.roll(line, 127, 1).astype(bf16)
+
     def rim_finish(field, turn):
         for number in range(8):
             there, _ = near(sizes, number)
@@ -309,9 +314,13 @@
         right = column(3, 6, 7)
         for y in range(height + 2):
             part = slice(y * 128, (y + 1) * 128)
-            line = field[own, part].astype(f32)
-            before = jnp.where(lane == 0, left[:, y : y + 1], pltpu.roll(line, 1, 1))
-            after = jnp.where(lane == 127, right[:, y : y + 1], pltpu.roll(line, 127, 1))
+            if y in (0, height + 1):
+                line = field[own, part].astype(f32)
+                before, after = pltpu.roll(line, 1, 1), pltpu.roll(line, 127, 1)
+            else:
+                before, after = field[0:MID, part].astype(f32), field[2 * MID :, part].astype(f32)
+            before = jnp.where(lane == 0, left[:, y : y + 1], before)
+            after = jnp.where(lane == 127, right[:, y : y + 1], after)
             field[0:MID, part] = before.astype(bf16)
             field[2 * MID :, part] = after.astype(bf16)
 

time: 62.6 us -> 59.3 us (0.947)
  Pallas kernels: 50.5 us -> 47.1 us
    pallas_call x1, Pallas kernels: 24.9 us -> 21.9 us  [lion_step(): pl.pallas_call(lambda *refs: lion_kernel(sizes, share, params, *refs), ou...]
where the time goes in v3:
time: 59.3 us; the launch traced here: 59.1 us
  Pallas kernels  47.1 us (79%)
  local copies, waits for them, and re-layouts  7.34 us (12%)
  between operations  2.8 us (5%)
  other arithmetic  1.82 us (3%)
    pallas_call x1, Pallas kernels, local(): pl.pallas_call(lambda *refs: bottleneck_kernel(sizes, height, total_tiles...  25.2 us
    pallas_call x1, Pallas kernels, lion_step(): pl.pallas_call(lambda *refs: lion_kernel(sizes, share, params, *refs), ou...  21.9 us
    unnamed x16, local copies, waits for them, and re-layouts  1.89 us
    slice x2, local copies, waits for them, and re-layouts, lion_step(): return (out[0], out[1], out[2], total[1, 0])  1.32 us

profile of v3, /device:TPU:0, one launch (start us, length us, event | category | flops | bytes accessed | tf_op | source)
XLA Modules:
  0.0 59.1 jit_solution(16404806647476131137)
XLA Ops:
  0.6 1.1 %convert.10 = bf16[141312]{0:T(1024)(128)(2,1)S(1)} convert(f32[141312]{0:T(1024)} %param.6) | non-fusion elementwise | flops 141312 | bytes 847872 | tf_op jit(solution)/shard_map/convert.7
  1.7 0.1 convert_element_type.31.refs_13_
  1.8 0.1 copy.16
  2.0 0.1 copy.19.refs_5_
  2.1 0.1 copy.20.refs_10_
  2.2 0.1 convert_element_type.28
  2.3 0.1 copy.13
  2.4 0.1 convert_element_type.29
  2.6 0.1 copy.15
  2.7 0.2 reshape.132.refs_6_
  2.9 0.1 convert_element_type.32
  3.0 0.1 copy.18
  3.1 0.2 reshape.134.refs_11_
  3.3 0.2 copy.14
  3.5 0.2 reshape.131.refs_4_
  3.6 0.2 copy.17
  3.8 0.2 reshape.133.refs_9_
  4.0 0.0 slice-start
  4.0 0.0 copy-start.2
  4.0 1.7 %copy.31 = bf16[32,8,24,128]{3,1,2,0:T(8,128)(2,1)S(1)} copy(bf16[32,8,24,128]{3,2,1,0:T(8,128)(2,1)} %bitcast.47) | data formatting | bytes 3145728
  5.7 0.0 slice-done
  5.7 0.1 slice.88
  5.9 0.0 copy-done.2
  5.9 0.1 iota_compare_fusion
  6.0 25.2 %shard_map.75 = (f32[256,64]{1,0:T(8,128)S(1)}, f32[192,192]{1,0:T(8,128)S(1)}, f32[64,256]{1,0:T(8,128)S(1)}, f32[256,64]{1,0:T(8,128)S(1)}, f32[192,192]{1,0:T...) custom-call(bf16[256,3072]{1,0:T(8,128)(2,1)S(1)} %bitcast.36, ...), custom_call_target="tpu_custom_call" | custom-call | tf_op jit(solution)/shard_map/pallas_call | solution.py:452
  31.2 0.1 copy.21
  31.3 0.1 copy.22
  31.4 0.1 reshape.137
  31.6 0.1 reshape.135
  31.6 0.0 copy-start.1
  31.7 0.0 copy-start
  31.8 0.1 reshape.139
  31.9 0.1 copy.23
  32.0 0.1 copy.24
  32.1 0.1 reshape.141
  32.3 0.1 reshape.143
  32.5 0.0 copy-done.1
  32.5 0.4 dynamic_update_slice.3
  32.8 0.0 copy-done
  32.9 0.5 slice.96
  33.4 0.6 %compare_select_fusion.refs_1_ = f32[1,128]{1,0:T(1,128)S(1)} fusion(f32[]{:T(128)} %bitcast.14), kind=kLoop, calls=%fused_computation.15 | loop fusion | flops 256 | bytes 516 | tf_op jit(solution)/shard_map/jit(_where)/select_n | solution.py:171
  34.0 21.9 %shard_map.76 = (f32[3,35,128]{2,1,0:T(8,128)S(1)}, f32[8,128]{1,0:T(8,128)S(1)}) custom-call(f32[1104,128]{1,0:T(8,128)S(1)} %bitcast.37, f32[1,128]{1,0:T(1,128)S(1)} %compare_select_fusion.refs_1_, f32[35,128]{1,0:T(8,128)S(1)} %bitcast.43, f32[35,128]{1,0:T(8,128)S(1)} %constant_dynamic-slice_fusion.refs_3_), custom_call_target="tpu_custom_call" | custom-call | tf_op jit(solution)/shard_map/pallas_call | solution.py:184
  56.0 0.8 %dynamic-slice_reduce_fusion = (f32[4416]{0:T(1024)}, f32[4416]{0:T(1024)}, f32[4416]{0:T(1024)}) fusion(f32[3,4480]{1,0:T(4,128)S(1)} %bitcast.55, s32[]{:T(128)S(6)} %add.29, s32[]{:T(128)S(6)} %select_n.24, s32[]{:T(128)S(6)} %add.28), kind=kLoop, calls=%fused_computation.4 | loop fusion | bytes 105996 | tf_op jit(solution)/shard_map/slice | solution.py:201
  56.8 0.5 slice.100
  (20 shorter events, 0.3 us)
Async XLA Ops:
  4.0 1.8 %slice-start = ((f32[141312]{0:T(1024)}), f32[2048]{0:T(1024)S(1)}, s32[]{:S(2)}) async-start(f32[141312]{0:T(1024)} %param.6), calls=%async_computation | async-start | bytes 16384 | tf_op jit(solution)/shard_map/slice | solution.py:34
  4.0 1.9 %copy-start.2 = (s32[1,1,2]{2,1,0:T(1,128)S(1)}, s32[1,1,2]{2,1,0:T(1,128)}, u32[]{:S(2)}) copy-start(s32[1,1,2]{2,1,0:T(1,128)} %param.5) | copy-start | bytes 28
  31.6 0.8 %copy-start.1 = (f32[4416]{0:T(1024)S(1)}, f32[4416]{0:T(1024)}, u32[]{:S(2)}) copy-start(f32[4416]{0:T(1024)} %param.7) | copy-start | bytes 52996
  31.7 1.2 %copy-start = (f32[141312]{0:T(1024)S(1)}, f32[141312]{0:T(1024)}, u32[]{:S(2)}) copy-start(f32[141312]{0:T(1024)} %param.6) | copy-start | bytes 1695748

commit v4 on v3

--- a/solution.py
+++ b/solution.py
@@ -63,6 +63,14 @@
     return plane, line
 
 
+def each(count, body):
+    if count <= 8:
+        for k in range(1, count):
+            body(k, 0)
+    else:
+        lax.fori_loop(1, count, body, 0)
+
+
 def greet(sizes):
     nrow, ncol, ndp = sizes
     plane, line = peers(sizes)
@@ -71,7 +79,7 @@
         def one(k, carry, target=target):
             pl.semaphore_signal(barrier, inc=1, device_id=target(k), device_id_type=MESH_ID)
             return carry
-        lax.fori_loop(1, count, one, 0)
+        each(count, one)
 
 
 def exchange(count, source, landing, target, send, recv):
@@ -88,8 +96,8 @@
         copy(k).wait()
         return carry
 
-    lax.fori_loop(1, count, start, 0)
-    lax.fori_loop(1, count, finish, 0)
+    each(count, start)
+    each(count, finish)
 
 
 def lion_kernel(sizes, share, params, flat_ref, loss_ref, mom_ref, wgt_ref, out_ref, total_ref,
@@ -135,7 +143,8 @@
     size = jnp.abs(mixed)
     part = jnp.sum(jnp.where(inside, size, 0.0), axis=0, keepdims=True)
     which = lax.broadcasted_iota(jnp.int32, (8, 128), 0)
-    mine[...] = jnp.where(which == 0, part, jnp.where(which == 1, loss_ref[...], 0.0))
+    at_loss = jnp.logical_and(which == 1, lax.broadcasted_iota(jnp.int32, (8, 128), 1) == 0)
+    mine[...] = jnp.where(which == 0, part, jnp.where(at_loss, loss_ref[...], 0.0))
     plane, line = peers(sizes)
     exchange(nrow * ncol, lambda k: mine, rp, plane, sems[6], sems[7])
     total = mine[...]
@@ -167,8 +176,6 @@
     spare = max(0, (count - 1) * share // 128 + rows - params // 128)
     wgt = jnp.pad(weights.reshape(-1, 128), ((0, spare), (0, 0)))
     wgt = lax.dynamic_slice_in_dim(wgt, first, rows, 0)
-    lane0 = jnp.arange(128)[None, :] == 0
-    loss_row = jnp.where(lane0, loss_part, 0.0)
     lo_n = split_col(ncol)
     hi_n = ncol // lo_n
     f32 = jnp.float32
@@ -196,7 +203,7 @@
         ] + sems,
         compiler_params=pltpu.CompilerParams(
             collective_id=0, has_side_effects=True, vmem_limit_bytes=40 * 1024 * 1024),
-    )(flat.reshape(-1, 128), loss_row, mom.reshape(rows, 128), wgt)
+    )(flat.reshape(-1, 128), loss_part, mom.reshape(rows, 128), wgt)
     out = lax.dynamic_slice_in_dim(out.reshape(3, rows * 128), skip, share, 1)
     return out[0], out[1], out[2], total[1, 0]
 
@@ -467,7 +474,7 @@
         gmid = gmid.reshape(3 * MID, 3, MID).transpose(1, 0, 2)
         flat += [gin.ravel(), gmid.ravel(), gout.ravel()]
     flat = jnp.concatenate(flat + [ghead[:, :CLASSES].ravel()])
-    new_weights, new_momentum, update, loss_total = lion_step(flat, loss[0, 0], weights, momentum)
+    new_weights, new_momentum, update, loss_total = lion_step(flat, loss, weights, momentum)
     return (new_weights, new_momentum, update, loss_total / total_tiles)
 
 

time: 59.3 us -> 58.1 us (0.980)
  other arithmetic: 1.82 us -> 1.17 us
    select_n x1 -> x0, other arithmetic: 0.65 us -> none  [lion_step(): loss_row = jnp.where(lane0, loss_part, 0.0)]
where the time goes in v4:
time: 58.1 us; the launch traced here: 57.8 us
  Pallas kernels  47.1 us (81%)
  local copies, waits for them, and re-layouts  6.82 us (12%)
  between operations  2.79 us (5%)
  other arithmetic  1.17 us (2%)
    pallas_call x1, Pallas kernels, local(): pl.pallas_call(lambda *refs: bottleneck_kernel(sizes, height, total_tiles...  25.2 us
    pallas_call x1, Pallas kernels, lion_step(): pl.pallas_call(lambda *refs: lion_kernel(sizes, share, params, *refs), ou...  21.8 us
    unnamed x16, local copies, waits for them, and re-layouts  1.89 us
    slice x2, local copies, waits for them, and re-layouts, lion_step(): return (out[0], out[1], out[2], total[1, 0])  1.32 us

profile of v4, /device:TPU:0, one launch (start us, length us, event | category | flops | bytes accessed | tf_op | source)
XLA Modules:
  0.0 57.8 jit_solution(9650868541670610032)
XLA Ops:
  0.6 1.1 %convert.10 = bf16[141312]{0:T(1024)(128)(2,1)S(1)} convert(f32[141312]{0:T(1024)} %param.6) | non-fusion elementwise | flops 141312 | bytes 847872 | tf_op jit(solution)/shard_map/convert.7
  1.7 0.1 convert_element_type.31.refs_13_
  1.8 0.1 copy.16
  2.0 0.1 copy.19.refs_5_
  2.1 0.1 copy.20.refs_10_
  2.2 0.1 convert_element_type.28
  2.3 0.1 copy.13
  2.4 0.1 convert_element_type.29
  2.6 0.1 copy.15
  2.7 0.2 reshape.120.refs_6_
  2.9 0.1 convert_element_type.32
  3.0 0.1 copy.18
  3.1 0.2 reshape.122.refs_11_
  3.3 0.2 copy.14
  3.5 0.2 reshape.119.refs_4_
  3.6 0.2 copy.17
  3.8 0.2 reshape.121.refs_9_
  4.0 0.0 slice-start
  4.0 0.0 copy-start.2
  4.0 1.7 %copy.31 = bf16[32,8,24,128]{3,1,2,0:T(8,128)(2,1)S(1)} copy(bf16[32,8,24,128]{3,2,1,0:T(8,128)(2,1)} %bitcast.46) | data formatting | bytes 3145728
  5.7 0.0 slice-done
  5.7 0.1 slice.85
  5.9 0.0 copy-done.2
  5.9 0.1 iota_compare_fusion
  6.0 25.2 %shard_map.75 = (f32[256,64]{1,0:T(8,128)S(1)}, f32[192,192]{1,0:T(8,128)S(1)}, f32[64,256]{1,0:T(8,128)S(1)}, f32[256,64]{1,0:T(8,128)S(1)}, f32[192,192]{1,0:T...) custom-call(bf16[256,3072]{1,0:T(8,128)(2,1)S(1)} %bitcast.35, ...), custom_call_target="tpu_custom_call" | custom-call | tf_op jit(solution)/shard_map/pallas_call | solution.py:459
  31.2 0.1 copy.21
  31.3 0.1 copy.22
  31.5 0.1 reshape.125
  31.6 0.1 reshape.123
  31.7 0.0 copy-start.1
  31.7 0.0 copy-start
  31.8 0.1 reshape.127
  31.9 0.1 copy.23
  32.0 0.1 copy.24
  32.1 0.1 reshape.129
  32.3 0.1 reshape.131
  32.5 0.0 copy-done.1
  32.5 0.4 dynamic_update_slice.3
  32.9 0.0 copy-done
  32.9 21.8 %shard_map.76 = (f32[3,35,128]{2,1,0:T(8,128)S(1)}, f32[8,128]{1,0:T(8,128)S(1)}) custom-call(f32[1104,128]{1,0:T(8,128)S(1)} %bitcast.36, f32[8,128]{1,0:T(8,128)S(1)} %get-tuple-element.21.refs_1_, f32[35,128]{1,0:T(8,128)S(1)} %bitcast.42, f32[35,128]{1,0:T(8,128)S(1)} %constant_dynamic-slice_fusion.refs_3_), custom_call_target="tpu_custom_call" | custom-call | tf_op jit(solution)/shard_map/pallas_call | solution.py:191
  54.7 0.8 %dynamic-slice_reduce_fusion = (f32[4416]{0:T(1024)}, f32[4416]{0:T(1024)}, f32[4416]{0:T(1024)}) fusion(f32[3,4480]{1,0:T(4,128)S(1)} %bitcast.54, s32[]{:T(128)S(6)} %add.29, s32[]{:T(128)S(6)} %select_n.19, s32[]{:T(128)S(6)} %add.28), kind=kLoop, calls=%fused_computation.4 | loop fusion | bytes 105996 | tf_op jit(solution)/shard_map/slice | solution.py:208
  55.6 0.5 slice.96
  (20 shorter events, 0.3 us)
Async XLA Ops:
  4.0 1.8 %slice-start = ((f32[141312]{0:T(1024)}), f32[2048]{0:T(1024)S(1)}, s32[]{:S(2)}) async-start(f32[141312]{0:T(1024)} %param.6), calls=%async_computation | async-start | bytes 16384 | tf_op jit(solution)/shard_map/slice | solution.py:34
  4.0 1.9 %copy-start.2 = (s32[1,1,2]{2,1,0:T(1,128)S(1)}, s32[1,1,2]{2,1,0:T(1,128)}, u32[]{:S(2)}) copy-start(s32[1,1,2]{2,1,0:T(1,128)} %param.5) | copy-start | bytes 28
  31.7 0.8 %copy-start.1 = (f32[4416]{0:T(1024)S(1)}, f32[4416]{0:T(1024)}, u32[]{:S(2)}) copy-start(f32[4416]{0:T(1024)} %param.7) | copy-start | bytes 52996
  31.7 1.2 %copy-start = (f32[141312]{0:T(1024)S(1)}, f32[141312]{0:T(1024)}, u32[]{:S(2)}) copy-start(f32[141312]{0:T(1024)} %param.6) | copy-start | bytes 1695748
